TPU v7x, 32 devices: a whole 2x2x4 slice. The times are simulated.
32 devices in a mesh: row: 8 (over y, x, core), col: 4 (over z).
Axes of the slice: x: 2, y: 2, z: 4, core: 2. Of those that a mesh axis runs over, the one named last changes fastest.
Arguments:
- inputs: bfloat16 [512, 16384], P('col', 'row'), may hold values from -6 to 6
- gate_weight: bfloat16 [16384, 26624], P('row', 'col'), may hold values from -0.0625 to 0.0625
- up_weight: bfloat16 [16384, 26624], P('row', 'col'), may hold values from -0.0625 to 0.0625
- gate_pattern: int32 [128, 208], P('row', 'col'), may hold values 0 or 1
- up_pattern: int32 [128, 208], P('row', 'col'), may hold values 0 or 1
- cotangent: bfloat16 [512, 26624], P('row', 'col'), may hold values from -6 to 6
Outputs:
- hidden: bfloat16 [512, 26624], P('row', 'col')
- input_grad: bfloat16 [512, 16384], P('col', 'row')
All inputs are finite; a program needn't handle non-finite values. No bound on the sum of `gate_pattern` or of `up_pattern` on one device may be relied on, other than what follows from the above.
Results may differ from a plain program's by a relative error of at most 0.039.
Values may be sent and summed in bfloat16 or wider, within the bound.
No kernel may reach another device: no remote copies, remote signals or barrier semaphores. Data moves between devices by JAX's collectives and lax.ppermute only.
A program may use at most 256 MiB of HBM per device.

v0:
```python
import functools

import jax
import jax.numpy as jnp
import numpy as np
from jax import lax
from jax.experimental import pallas as pl
from jax.experimental.pallas import tpu as pltpu
from jax.sharding import PartitionSpec as P

BLOCK = 128
FORWARD = (2, 3, 4, 4)
BACKWARD = (5, 8)
FEATURE_PARTS = 2
VMEM_BYTES = 48 * 1024 * 1024
ANY = pl.BlockSpec(memory_space=pl.ANY)
COST = pl.CostEstimate(flops=1, bytes_accessed=1, transcendentals=0)


def masked(w_ref, f_ref):
    rows, columns = w_ref.shape
    flags = f_ref[...].reshape(rows // BLOCK, 1, columns)
    return (w_ref[...].reshape(rows // BLOCK, BLOCK, columns) * flags).reshape(rows, columns)


def then(array, *others):
    return lax.optimization_barrier((array, *others))[0]


class Cube:
    def __init__(self, size):
        self.size = size
        self.half = size // 2
        rising = [1 << b for b in range(1, size.bit_length() - 1)]
        self.dims = (rising, rising[::-1])

    def offset(self, parity, slot):
        dims = self.dims[parity]
        digits = [slot >> (len(dims) - 1 - i) & 1 for i in range(len(dims))]
        return int(np.bitwise_xor.reduce([0] + [d for d, on in zip(dims, digits) if on]))

    def owner(self, me, slot):
        if slot >= self.half:
            me, slot = me ^ 1, slot - self.half
        return me ^ self.offset(me & 1, slot)

    def step(self, array, i):
        perm = [(r, r ^ self.dims[r & 1][i]) for r in range(self.size)]
        return lax.ppermute(array, "row", perm)

    def sibling(self, array):
        return lax.ppermute(array, "row", [(r, r ^ 1) for r in range(self.size)])


def places(cube, n_col):
    ratio = cube.size // n_col
    table = np.zeros((cube.size, n_col, cube.size), np.int32)
    for me in range(cube.size):
        for z in range(n_col):
            for slot in range(cube.size):
                d = cube.owner(me, slot)
                table[me, z, slot] = ratio * ((d // ratio) ^ z) + d % ratio
    return table


def copy_all(copies):
    for copy in copies:
        copy.start()
    for copy in copies:
        copy.wait()


def forward_kernel(n_x, n_after, slots, *refs):
    x_refs, refs = refs[:n_x], refs[n_x:]
    wg_ref, wu_ref, fg_ref, fu_ref = refs[:4]
    keep_ref, send_ref, x_all, sem = refs[4 + n_after :]
    half = keep_ref.shape[1]
    shares = slots.shape[0]
    share = 2 * half // shares
    ratio = shares // n_x

    @pl.when(pl.program_id(0) == 0)
    def _():
        copies = []
        for k in range(n_x):
            for c in range(ratio):
                place = k * ratio + c
                row = pl.multiple_of(slots[place] * share, share)
                copies.append(
                    pltpu.make_async_copy(
                        x_refs[k].at[pl.ds(c * share, share), :],
                        x_all.at[pl.ds(row, share), :],
                        sem.at[place],
                    )
                )
        copy_all(copies)

    for n, (w_ref, f_ref) in enumerate(((wg_ref, fg_ref), (wu_ref, fu_ref))):
        out = jnp.dot(x_all[...], masked(w_ref, f_ref), preferred_element_type=jnp.float32)
        out = out.astype(jnp.bfloat16)
        keep_ref[n] = out[:half]
        send_ref[n] = out[half:]


def forward(slots, xs, weights, flags, first, tiles, tile, after):
    depth = weights[0].shape[0]
    rows = len(xs) * xs[0].shape[0]
    w_spec = pl.BlockSpec((depth, tile), lambda i, s: (0, first + i))
    f_spec = pl.BlockSpec((*flags[0].shape[:2], tile), lambda i, s: (0, 0, first + i))
    o_spec = pl.BlockSpec((2, rows // 2, tile), lambda i, s: (0, 0, i))
    out = jax.ShapeDtypeStruct((2, rows // 2, tiles * tile), jnp.bfloat16)
    return pl.pallas_call(
        functools.partial(forward_kernel, len(xs), len(after)),
        grid_spec=pltpu.PrefetchScalarGridSpec(
            num_scalar_prefetch=1,
            grid=(tiles,),
            in_specs=[ANY] * len(xs) + [w_spec] * 2 + [f_spec] * 2 + [ANY] * len(after),
            out_specs=[o_spec, o_spec],
            scratch_shapes=[
                pltpu.VMEM((rows, depth), jnp.bfloat16),
                pltpu.SemaphoreType.DMA((slots.shape[0],)),
            ],
        ),
        out_shape=[out, out],
        compiler_params=pltpu.CompilerParams(vmem_limit_bytes=VMEM_BYTES),
        cost_estimate=pl.CostEstimate(
            flops=8 * rows * depth * tiles * tile,
            bytes_accessed=4 * depth * tiles * tile,
            transcendentals=0,
        ),
    )(slots, *xs, *weights, *flags, *after)


def derivatives_kernel(first, layout, n_terms, *refs):
    sources, cot_ref = refs[: len(layout) * n_terms], refs[len(layout) * n_terms]
    h_ref, g_ref = refs[-4 - n_terms : -2 - n_terms]
    held = refs[-2 - n_terms : -2]
    cot, sem = refs[-2:]
    share, columns = h_ref.shape
    copies = []
    for m, (source, place, width) in enumerate(layout):
        for n in range(n_terms):
            copies.append(
                pltpu.make_async_copy(
                    sources[m * n_terms + n].at[:, pl.ds(0, share), pl.ds(source, width)],
                    held[n].at[:, :, pl.ds(place, width)],
                    sem.at[m * n_terms + n],
                )
            )
    copies.append(
        pltpu.make_async_copy(
            cot_ref.at[:, pl.ds(first, columns)], cot, sem.at[len(layout) * n_terms]
        )
    )
    copy_all(copies)
    step = 256
    for c in range(0, columns, step):
        at = slice(c, c + step)
        gate_sum = sum(wide(v[0, :, at]) for v in held)
        up_sum = sum(wide(v[1, :, at]) for v in held)
        cotangent = wide(cot[:, at])
        sigmoid_gate = jax.nn.sigmoid(gate_sum)
        activated = gate_sum * sigmoid_gate
        h_ref[:, at] = (activated * up_sum).astype(jnp.bfloat16)
        g_ref[0, :, at] = (
            cotangent * up_sum * sigmoid_gate * (1.0 + gate_sum * (1.0 - sigmoid_gate))
        ).astype(jnp.bfloat16)
        g_ref[1, :, at] = (cotangent * activated).astype(jnp.bfloat16)


def derivatives(layout, terms, cotangent, first, columns, after):
    share = cotangent.shape[0]
    n_terms = len(terms[0])
    return pl.pallas_call(
        functools.partial(derivatives_kernel, first, layout, n_terms),
        in_specs=[ANY] * (len(layout) * n_terms + 1 + len(after)),
        out_specs=[pl.BlockSpec(memory_space=pltpu.VMEM)] * 2,
        out_shape=[
            jax.ShapeDtypeStruct((share, columns), jnp.bfloat16),
            jax.ShapeDtypeStruct((2, share, columns), jnp.bfloat16),
        ],
        scratch_shapes=[pltpu.VMEM((2, share, columns), jnp.bfloat16)] * n_terms
        + [
            pltpu.VMEM((share, columns), jnp.bfloat16),
            pltpu.SemaphoreType.DMA((len(layout) * n_terms + 1,)),
        ],
        compiler_params=pltpu.CompilerParams(vmem_limit_bytes=VMEM_BYTES),
        cost_estimate=COST,
    )(*sum(terms, []), cotangent, *after)


def backward_kernel(n_out, steps, chained, n_after, part, where, *refs):
    n_slots = where.shape[0]
    g_refs, refs = refs[:n_slots], refs[n_slots:]
    (wg_ref, wu_ref, fg_ref, fu_ref), refs = refs[:4], refs[4:]
    if chained:
        carry_ref, refs = refs[0], refs[1:]
    refs = refs[n_after:]
    o_refs = refs[:n_out]
    g_all, acc, both, sem = refs[n_out:]
    i = pl.program_id(0)
    tile = wg_ref.shape[1]
    depth, rows = acc.shape
    share = rows // n_slots

    @pl.when(i == 0)
    def _():
        copies = []
        for slot in range(n_slots):
            row = pl.multiple_of(where[slot] * share, share)
            copies.append(
                pltpu.make_async_copy(
                    g_refs[slot], g_all.at[:, pl.ds(row, share), :], sem.at[slot]
                )
            )
        if chained:
            copies.append(
                pltpu.make_async_copy(
                    carry_ref.at[pl.ds(part * depth, depth), :], acc, sem.at[n_slots]
                )
            )
        else:
            acc[...] = jnp.zeros_like(acc)
        copy_all(copies)

    columns = pl.ds(pl.multiple_of(i * tile, tile), tile)
    both[:, :tile] = masked(wg_ref, fg_ref)
    both[:, tile:] = masked(wu_ref, fu_ref)
    acc[...] += lax.dot_general(
        both[...],
        jnp.concatenate([g_all[0, :, columns], g_all[1, :, columns]], axis=1),
        (((1,), (1,)), ((), ())),
        preferred_element_type=jnp.float32,
    )

    @pl.when(i == steps - 1)
    def _():
        if n_out == 1:
            copy_all([pltpu.make_async_copy(acc, o_refs[0], sem.at[0])])
        else:
            for k in range(n_out):
                size = rows // n_out
                o_refs[k][...] = acc[:, k * size : (k + 1) * size].T.astype(jnp.bfloat16)


def backward(carry, where, pieces, weights, flags, first, tile, part, planes, after):
    n_slots = where.shape[0]
    width = pieces[0].shape[2]
    rows = pieces[0].shape[1] * n_slots
    depth = weights[0].shape[0]
    f_parts = FEATURE_PARTS
    if part is not None:
        depth, f_parts = depth // FEATURE_PARTS, 1
    row = part or 0
    tiles = width // tile
    w_spec = pl.BlockSpec((depth, tile), lambda i, s: (row, first + i))
    f_spec = pl.BlockSpec(
        (f_parts, flags[0].shape[1], tile), lambda i, s: (row, 0, first + i)
    )
    if planes:
        out_specs = [pl.BlockSpec((rows // planes, depth), lambda i, s: (0, 0))] * planes
        out_shape = [jax.ShapeDtypeStruct((rows // planes, depth), jnp.bfloat16)] * planes
    else:
        out_specs = [ANY]
        out_shape = [jax.ShapeDtypeStruct((depth, rows), jnp.float32)]
    chained = carry is not None
    return pl.pallas_call(
        functools.partial(
            backward_kernel, len(out_shape), tiles, chained, len(after), part
        ),
        grid_spec=pltpu.PrefetchScalarGridSpec(
            num_scalar_prefetch=1,
            grid=(tiles,),
            in_specs=[ANY] * n_slots + [w_spec] * 2 + [f_spec] * 2 + [ANY] * (chained + len(after)),
            out_specs=out_specs,
            scratch_shapes=[
                pltpu.VMEM((2, rows, width), jnp.bfloat16),
                pltpu.VMEM((depth, rows), jnp.float32),
                pltpu.VMEM((depth, 2 * tile), jnp.bfloat16),
                pltpu.SemaphoreType.DMA((n_slots + 1,)),
            ],
        ),
        out_shape=out_shape,
        compiler_params=pltpu.CompilerParams(vmem_limit_bytes=VMEM_BYTES),
        cost_estimate=pl.CostEstimate(
            flops=6 * rows * depth * width,
            bytes_accessed=4 * depth * width,
            transcendentals=0,
        ),
    )(where, *pieces, *weights, *flags, *((carry,) if chained else ()), *after)


def wide(array):
    return array.astype(jnp.float32)


class ReduceScatter:
    def __init__(self, cube, keep, send):
        self.cube = cube
        self.terms = [keep, cube.sibling(send)]
        self.rows = keep.shape[1]

    def exchange(self, i, after):
        self.rows //= 2
        self.terms[0] = then(self.terms[0], *after)
        rows = self.rows
        moved = sum(wide(t[:, rows : 2 * rows]) for t in self.terms).astype(jnp.bfloat16)
        self.terms.append(self.cube.step(moved, i))
        if i == 0:
            self.first = self.terms[-1]
        return moved


class AllGather:
    def __init__(self, cube, own, *after):
        self.cube = cube
        n_dims = len(cube.dims[0])
        own = then(own, *after)
        self.pieces = [own] + [cube.step(own, n_dims - 1 - i) for i in range(n_dims)]

    def finish(self, *after):
        cube = self.cube
        n_dims = len(cube.dims[0])
        pieces = {0: self.pieces[0]}
        for i in range(n_dims):
            pieces[1 << i] = self.pieces[1 + i]
        pieces = {slot: then(p, *after) for slot, p in pieces.items()}
        for slot in range(1, cube.half):
            if slot not in pieces:
                low = slot & -slot
                pieces[slot] = cube.step(pieces[slot ^ low], n_dims - low.bit_length())
        pieces = [pieces[slot] for slot in range(cube.half)]
        return pieces + [cube.sibling(p) for p in pieces]


def flip(array, bit, size):
    return lax.ppermute(array, "col", [(z, z ^ bit) for z in range(size)])


def gather_planes(x, n_col):
    xs = [x]
    for k in range(1, n_col):
        low = k & -k
        xs.append(flip(xs[k ^ low], low, n_col))
    return xs


def sum_planes(parts, n_col, direct, after):
    terms = [wide(p) for p in parts]
    arrived = list(after)
    for k in range(n_col - 1, 0, -1):
        low = k if direct else k & -k
        sent = terms[k].astype(jnp.bfloat16)
        if not direct:
            sent = then(sent, *arrived)
        moved = flip(sent, low, n_col)
        if direct or low != k:
            arrived.append(moved)
        terms[k ^ low] = terms[k ^ low] + wide(moved)
    return terms[0].astype(jnp.bfloat16), arrived


def shards(cube, n_col, inputs, gate_weight, up_weight, gate_pattern, up_pattern, cotangent):
    depth, local_hidden = gate_weight.shape
    share = cotangent.shape[0]
    tile = local_hidden // sum(BACKWARD)
    weights = (gate_weight, up_weight)
    flags = [
        jnp.repeat(p.astype(jnp.bfloat16), BLOCK, axis=1).reshape(
            FEATURE_PARTS, -1, local_hidden
        )
        for p in (gate_pattern, up_pattern)
    ]
    table = places(cube, n_col)
    row, col = lax.axis_index("row"), lax.axis_index("col")
    where = jnp.asarray(table)[row, col]
    slots = jnp.asarray(np.argsort(table, axis=-1).astype(np.int32))[row, col]

    xs = gather_planes(inputs, n_col)
    units = list(zip(np.cumsum((0,) + FORWARD).tolist(), FORWARD))
    sums, after, moved = [], {}, []
    for n, (first, tiles) in enumerate(units):
        keep, send = forward(
            slots, xs, weights, flags, first, tiles, tile, after.pop(n, [])
        )
        sums.append(ReduceScatter(cube, keep, send))
        after.setdefault(n + 1, []).append(keep)
        moved.append([])
        for i in range(len(cube.dims[0])):
            before = sums[n - 2].terms[-1:] if i == 0 and n > 2 else []
            moved[n].append(sums[n].exchange(i, before))
            after.setdefault(n + 2 + i, []).append(moved[n][-1])
    first_moved = [m[0] for m in moved]

    hidden, gathers, owns = [], [], []
    starts = [sum(BACKWARD[:n]) for n in range(len(BACKWARD))]
    for first, tiles in zip(starts, BACKWARD):
        layout, terms = [], []
        for (start, width), unit in zip(units, sums):
            low, high = max(first, start), min(first + tiles, start + width)
            if low < high:
                layout.append(((low - start) * tile, (low - first) * tile, (high - low) * tile))
                terms.append(unit.terms)
        h, own = derivatives(
            layout, terms, cotangent, first * tile, tiles * tile, owns[-1:] or first_moved
        )
        hidden.append(h)
        owns.append(own)
        gathers.append(AllGather(cube, own))
    carry = backward(
        None, where, gathers[0].finish(), weights, flags, 0, tile, None, 0, owns[1:]
    )
    pieces = gathers[1].finish(*carry)
    input_grad, arrived, parts = [], [], []
    for part in range(FEATURE_PARTS):
        parts = backward(
            carry[0],
            where,
            pieces,
            weights,
            flags,
            starts[1],
            tile,
            part,
            n_col,
            parts[:1],
        )
        total, arrived = sum_planes(parts, n_col, part < FEATURE_PARTS - 1, arrived)
        input_grad.append(total)
    return jnp.concatenate(hidden, axis=1), jnp.concatenate(input_grad, axis=1)


def solution(mesh):
    placed = (
        P("col", "row"),
        P("row", "col"),
        P("row", "col"),
        P("row", "col"),
        P("row", "col"),
        P("row", "col"),
    )
    return jax.shard_map(
        functools.partial(shards, Cube(mesh.shape["row"]), mesh.shape["col"]),
        mesh=mesh,
        in_specs=placed,
        out_specs=(P("row", "col"), P("col", "row")),
        check_vma=False,
    )
```

profile of v0, /device:TPU:0, one launch (start us, length us, event | category | flops | bytes accessed | tf_op | source)
XLA Modules:
  0.0 277.5 jit_solution(18040878894947065774)
XLA Ops:
  0.6 4.1 %collective-permute-start.1 = (bf16[128,2048]{1,0:T(8,128)(2,1)}, bf16[128,2048]{1,0:T(8,128)(2,1)S(1)}, u32[]{:S(2)}, u32[]{:S(2)}) collective-permute-start(bf16[128,2048]{1,0:T(8,128)(2,1)} %refs_0_.7), channel_id=1, source_target_pairs={{0,2},{1,3},{2,0},{3,1},{4,6},{5,7},{6,4},{7,5},{8,10},{9,11},{10,... | collective-permute-start | bytes 1572872 | tf_op jit(solution)/shard_map/ppermute | solution.py:337
  4.7 1.6 collective-permute-start
  6.3 21.9 %collective-permute-done.1.refs_2_ = bf16[128,2048]{1,0:T(8,128)(2,1)S(1)} collective-permute-done((bf16[128,2048]{1,0:T(8,128)(2,1)}, bf16[128,2048]{1,0:T(8,128)(2,1)S(1)}, u32[]{:S(2)}, u32[]{:S(2)}) %collective-permute-start.1) | collective-permute-done | bytes 524320 | tf_op jit(solution)/shard_map/ppermute | solution.py:337
  31.7 9.6 %collective-permute-done.2.refs_3_ = bf16[128,2048]{1,0:T(8,128)(2,1)S(1)} collective-permute-done((bf16[128,2048]{1,0:T(8,128)(2,1)S(1)}, bf16[128,2048]{1,0:T(8,128)(2,1)S(1)}, u32[]{:S(2)}, u32[]{:S(2)}) %collective-permute-start.2) | collective-permute-done | bytes 524320 | tf_op jit(solution)/shard_map/ppermute | solution.py:337
  42.3 7.9 %shard_map.95 = (bf16[2,256,1024]{2,1,0:T(8,128)(2,1)S(1)}, bf16[2,256,1024]{2,1,0:T(8,128)(2,1)S(1)}) custom-call(s32[8]{0:T(128)S(1)} %dynamic-slice_bitcast_fusion.1.slots, bf16[128,2048]{1,0:T(8,128)(2,1)S(1)} %copy-done.5, bf16[128,2048]{1,0:T(8,128)(2,1)S(1)} %collective-permute-done.refs_1_, bf16[128,2048]{1,0:T(8,128)(2,1)S(1)} %collective-permute-done.1.refs_2_, ...), custom_call_target="tpu_custom_call" | custom-call | flops 8589934592 | bytes 8388608 | tf_op jit(solution)/shard_map/pallas_call | solution.py:112
  50.3 11.1 %shard_map.96 = (bf16[2,256,1536]{2,1,0:T(8,128)(2,1)S(1)}, bf16[2,256,1536]{2,1,0:T(8,128)(2,1)}) custom-call(s32[8]{0:T(128)S(1)} %dynamic-slice_bitcast_fusion.1.slots, bf16[128,2048]{1,0:T(8,128)(2,1)S(1)} %copy-done.5, bf16[128,2048]{1,0:T(8,128)(2,1)S(1)} %collective-permute-done.refs_1_, bf16[128,2048]{1,0:T(8,128)(2,1)S(1)} %collective-permute-done.1.refs_2_, ...), custom_call_target="tpu_custom_call" | custom-call | flops 12884901888 | bytes 12582912 | tf_op jit(solution)/shard_map/pallas_call | solution.py:112
  63.4 13.7 %shard_map.97 = (bf16[2,256,2048]{2,1,0:T(8,128)(2,1)}, bf16[2,256,2048]{2,1,0:T(8,128)(2,1)}) custom-call(s32[8]{0:T(128)S(1)} %dynamic-slice_bitcast_fusion.1.slots, bf16[128,2048]{1,0:T(8,128)(2,1)S(1)} %copy-done.5, bf16[128,2048]{1,0:T(8,128)(2,1)S(1)} %collective-permute-done.refs_1_, bf16[128,2048]{1,0:T(8,128)(2,1)S(1)} %collective-permute-done.1.refs_2_, ...), custom_call_target="tpu_custom_call" | custom-call | flops 17179869184 | bytes 16777216 | tf_op jit(solution)/shard_map/pallas_call | solution.py:112
  78.9 13.5 %shard_map.98 = (bf16[2,256,2048]{2,1,0:T(8,128)(2,1)S(1)}, bf16[2,256,2048]{2,1,0:T(8,128)(2,1)}) custom-call(s32[8]{0:T(128)S(1)} %dynamic-slice_bitcast_fusion.1.slots, bf16[128,2048]{1,0:T(8,128)(2,1)S(1)} %copy-done.5, bf16[128,2048]{1,0:T(8,128)(2,1)S(1)} %collective-permute-done.refs_1_, bf16[128,2048]{1,0:T(8,128)(2,1)S(1)} %collective-permute-done.1.refs_2_, ...), custom_call_target="tpu_custom_call" | custom-call | flops 17179869184 | bytes 16777216 | tf_op jit(solution)/shard_map/pallas_call | solution.py:112
  93.8 1.5 collective-permute-start.5
  95.3 5.8 %collective-permute-done.8.refs_7_ = bf16[2,64,1536]{2,1,0:T(8,128)(2,1)S(1)} collective-permute-done((bf16[2,64,1536]{2,1,0:T(8,128)(2,1)S(1)}, bf16[2,64,1536]{2,1,0:T(8,128)(2,1)S(1)}, u32[]{:S(2)}, u32[]{:S(2)}) %collective-permute-start.8) | collective-permute-done | bytes 393248 | tf_op jit(solution)/shard_map/ppermute | solution.py:49
  101.0 1.6 add_convert_fusion.1.refs_11_
  103.3 1.4 add_convert_fusion.refs_12_
  105.0 2.0 shard_map.99
  107.0 1.6 collective-permute-start.16
  110.4 21.2 %collective-permute-done.16.refs_2_ = bf16[2,64,2560]{2,1,0:T(8,128)(2,1)S(1)} collective-permute-done((bf16[2,64,2560]{2,1,0:T(8,128)(2,1)S(1)}, bf16[2,64,2560]{2,1,0:T(8,128)(2,1)S(1)}, u32[]{:S(2)}, u32[]{:S(2)}) %collective-permute-start.16) | collective-permute-done | bytes 655392 | tf_op jit(solution)/shard_map/ppermute | solution.py:49
  132.1 1.4 add_convert_fusion.4
  133.5 1.6 collective-permute-start.12
  135.6 17.4 %collective-permute-done.13.refs_6_ = bf16[2,128,2048]{2,1,0:T(8,128)(2,1)S(1)} collective-permute-done((bf16[2,128,2048]{2,1,0:T(8,128)(2,1)S(1)}, bf16[2,128,2048]{2,1,0:T(8,128)(2,1)S(1)}, u32[]{:S(2)}, u32[]{:S(2)}) %collective-permute-start.13) | collective-permute-done | bytes 1048608 | tf_op jit(solution)/shard_map/ppermute | solution.py:49
  155.8 8.3 %collective-permute-done.14.refs_7_ = bf16[2,64,2048]{2,1,0:T(8,128)(2,1)S(1)} collective-permute-done((bf16[2,64,2048]{2,1,0:T(8,128)(2,1)S(1)}, bf16[2,64,2048]{2,1,0:T(8,128)(2,1)S(1)}, u32[]{:S(2)}, u32[]{:S(2)}) %collective-permute-start.14) | collective-permute-done | bytes 524320 | tf_op jit(solution)/shard_map/ppermute | solution.py:49
  164.1 2.6 shard_map.100
  168.3 18.2 %shard_map.101.refs_12_ = f32[2048,512]{1,0:T(8,128)} custom-call(s32[8]{0:T(128)S(1)} %dynamic-slice_bitcast_fusion.where, bf16[2,64,2560]{2,1,0:T(8,128)(2,1)S(1)} %get-tuple-element.39.refs_9_.refs_0_, bf16[2,64,2560]{2,1,0:T(8,128)(2,1)S(1)} %collective-permute-done.15.refs_1_, bf16[2,64,2560]{2,1,0:T(8,128)(2,1)S(1)} %collective-permute-done.16.refs_2_, ...), custom_call_target="tpu_custom_call" | custom-call | flops 16106127360 | bytes 20971520 | tf_op jit(solution)/shard_map/pallas_call | solution.py:267
  186.5 5.1 %collective-permute-done.23.refs_2_ = bf16[2,64,4096]{2,1,0:T(8,128)(2,1)S(1)} collective-permute-done((bf16[2,64,4096]{2,1,0:T(8,128)(2,1)S(1)}, bf16[2,64,4096]{2,1,0:T(8,128)(2,1)S(1)}, u32[]{:S(2)}, u32[]{:S(2)}) %collective-permute-start.23) | collective-permute-done | bytes 1048608 | tf_op jit(solution)/shard_map/ppermute | solution.py:49
  191.6 1.4 collective-permute-start.24
  193.5 12.9 %collective-permute-done.24.refs_3_ = bf16[2,64,4096]{2,1,0:T(8,128)(2,1)S(1)} collective-permute-done((bf16[2,64,4096]{2,1,0:T(8,128)(2,1)S(1)}, bf16[2,64,4096]{2,1,0:T(8,128)(2,1)S(1)}, u32[]{:S(2)}, u32[]{:S(2)}) %collective-permute-start.24) | collective-permute-done | bytes 1048608 | tf_op jit(solution)/shard_map/ppermute | solution.py:49
  206.5 2.6 collective-permute-done.28.refs_7_
  211.3 17.0 %shard_map.102 = (bf16[128,1024]{1,0:T(8,128)(2,1)S(1)}, bf16[128,1024]{1,0:T(8,128)(2,1)S(1)}, bf16[128,1024]{1,0:T(8,128)(2,1)S(1)}, bf16[128,1024]{1,0:T(8,128)(2,1)S(1)}) custom-call(s32[8]{0:T(128)S(1)} %dynamic-slice_bitcast_fusion.where, bf16[2,64,4096]{2,1,0:T(8,128)(2,1)S(1)} %copy-done.1, bf16[2,64,4096]{2,1,0:T(8,128)(2,1)S(1)} %collective-permute-done.22.refs_1_, ...), custom_call_target="tpu_custom_call" | custom-call | flops 12884901888 | bytes 16777216 | tf_op jit(solution)/shard_map/pallas_call | solution.py:267
  228.3 4.5 %collective-permute-start.29 = (bf16[128,1024]{1,0:T(8,128)(2,1)S(1)}, bf16[128,1024]{1,0:T(8,128)(2,1)S(1)}, u32[]{:S(2)}, u32[]{:S(2)}) collective-permute-start(bf16[128,1024]{1,0:T(8,128)(2,1)S(1)} %get-tuple-element.46), channel_id=1, source_target_pairs={{0,3},{1,2},{2,1},{3,0},{4,7},{5,6},{6,5},{7,4},{8,11},{9,10},{10,... | collective-permute-start | bytes 786440 | tf_op jit(solution)/shard_map/ppermute | solution.py:337
  233.5 17.0 %shard_map.103 = (bf16[128,1024]{1,0:T(8,128)(2,1)S(1)}, bf16[128,1024]{1,0:T(8,128)(2,1)S(1)}, bf16[128,1024]{1,0:T(8,128)(2,1)S(1)}, bf16[128,1024]{1,0:T(8,128)(2,1)S(1)}) custom-call(s32[8]{0:T(128)S(1)} %dynamic-slice_bitcast_fusion.where, bf16[2,64,4096]{2,1,0:T(8,128)(2,1)S(1)} %copy-done.1, bf16[2,64,4096]{2,1,0:T(8,128)(2,1)S(1)} %collective-permute-done.22.refs_1_, ...), custom_call_target="tpu_custom_call" | custom-call | flops 12884901888 | bytes 16777216 | tf_op jit(solution)/shard_map/pallas_call | solution.py:267
  250.5 4.6 %collective-permute-done.30 = bf16[128,1024]{1,0:T(8,128)(2,1)S(1)} collective-permute-done((bf16[128,1024]{1,0:T(8,128)(2,1)S(1)}, bf16[128,1024]{1,0:T(8,128)(2,1)S(1)}, u32[]{:S(2)}, u32[]{:S(2)}) %collective-permute-start.30) | collective-permute-done | bytes 262176 | tf_op jit(solution)/shard_map/ppermute | solution.py:337
  255.1 7.8 %collective-permute-done.32 = bf16[128,1024]{1,0:T(8,128)(2,1)S(1)} collective-permute-done((bf16[128,1024]{1,0:T(8,128)(2,1)S(1)}, bf16[128,1024]{1,0:T(8,128)(2,1)S(1)}, u32[]{:S(2)}, u32[]{:S(2)}) %collective-permute-start.32) | collective-permute-done | bytes 262176 | tf_op jit(solution)/shard_map/ppermute | solution.py:337
  264.2 1.7 collective-permute-start.34
  267.1 9.4 %collective-permute-done.33 = bf16[128,1024]{1,0:T(8,128)(2,1)S(1)} collective-permute-done((bf16[128,1024]{1,0:T(8,128)(2,1)S(1)}, bf16[128,1024]{1,0:T(8,128)(2,1)S(1)}, u32[]{:S(2)}, u32[]{:S(2)}) %collective-permute-start.33) | collective-permute-done | bytes 262176 | tf_op jit(solution)/shard_map/ppermute | solution.py:337
  (100 shorter events, 24.4 us)
Async XLA Ops:
  0.6 27.6 %collective-permute-start.1 = (bf16[128,2048]{1,0:T(8,128)(2,1)}, bf16[128,2048]{1,0:T(8,128)(2,1)S(1)}, u32[]{:S(2)}, u32[]{:S(2)}) collective-permute-start(bf16[128,2048]{1,0:T(8,128)(2,1)} %refs_0_.7), channel_id=1, source_target_pairs={{0,2},{1,3},{2,0},{3,1},{4,6},{5,7},{6,4},{7,5},{8,10},{9,11},{10,... | collective-permute-start | bytes 1572872 | tf_op jit(solution)/shard_map/ppermute | solution.py:337
  4.7 26.9 %collective-permute-start = (bf16[128,2048]{1,0:T(8,128)(2,1)}, bf16[128,2048]{1,0:T(8,128)(2,1)S(1)}, u32[]{:S(2)}, u32[]{:S(2)}) collective-permute-start(bf16[128,2048]{1,0:T(8,128)(2,1)} %refs_0_.7), channel_id=1, source_target_pairs={{0,1},{1,0},{2,3},{3,2},{4,5},{5,4},{6,7},{7,6},{8,9},{9,8},{10,11... | collective-permute-start | bytes 1572872 | tf_op jit(solution)/shard_map/ppermute | solution.py:337
  28.2 13.0 %collective-permute-start.2 = (bf16[128,2048]{1,0:T(8,128)(2,1)S(1)}, bf16[128,2048]{1,0:T(8,128)(2,1)S(1)}, u32[]{:S(2)}, u32[]{:S(2)}) collective-permute-start(bf16[128,2048]{1,0:T(8,128)(2,1)S(1)} %collective-permute-done.1.refs_2_), channel_id=1, source_target_pairs={{0,1},{1,0},{2,3},{3,2},{4,5},{5,4},{6,7},{7,6},{8,9},{9,8},{10,11... | collective-permute-start | bytes 1572872 | tf_op jit(solution)/shard_map/ppermute | solution.py:337
  50.2 11.7 %collective-permute-start.3 = (bf16[2,256,1024]{2,1,0:T(8,128)(2,1)S(1)}, bf16[2,256,1024]{2,1,0:T(8,128)(2,1)S(1)}, u32[]{:S(2)}, u32[]{:S(2)}) collective-permute-start(bf16[2,256,1024]{2,1,0:T(8,128)(2,1)S(1)} %get-tuple-element.30), channel_id=1, source_target_pairs={{0,4},{4,0},{8,12},{12,8},{16,20},{20,16},{24,28},{28,24},{1,5},{5... | collective-permute-start | bytes 3145736 | tf_op jit(solution)/shard_map/ppermute | solution.py:52
  61.4 15.9 %collective-permute-start.6 = (bf16[2,256,1536]{2,1,0:T(8,128)(2,1)}, bf16[2,256,1536]{2,1,0:T(8,128)(2,1)S(1)}, u32[]{:S(2)}, u32[]{:S(2)}) collective-permute-start(bf16[2,256,1536]{2,1,0:T(8,128)(2,1)} %get-tuple-element.32), channel_id=1, source_target_pairs={{0,4},{4,0},{8,12},{12,8},{16,20},{20,16},{24,28},{28,24},{1,5},{5... | collective-permute-start | bytes 4718600 | tf_op jit(solution)/shard_map/ppermute | solution.py:52
  62.1 16.7 %collective-permute-start.4 = (bf16[2,128,1024]{2,1,0:T(8,128)(2,1)S(1)}, bf16[2,128,1024]{2,1,0:T(8,128)(2,1)S(1)}, u32[]{:S(2)}, u32[]{:S(2)}) collective-permute-start(bf16[2,128,1024]{2,1,0:T(8,128)(2,1)S(1)} %add_convert_fusion.5.refs_8_.refs_9_), channel_id=1, source_target_pairs={{0,8},{4,20},{8,0},{12,28},{16,24},{20,4},{24,16},{28,12},{1,9},{5... | collective-permute-start | bytes 1572872 | tf_op jit(solution)/shard_map/ppermute | solution.py:49
  77.2 23.8 %collective-permute-start.9 = (bf16[2,256,2048]{2,1,0:T(8,128)(2,1)}, bf16[2,256,2048]{2,1,0:T(8,128)(2,1)}, u32[]{:S(2)}, u32[]{:S(2)}) collective-permute-start(bf16[2,256,2048]{2,1,0:T(8,128)(2,1)} %get-tuple-element.34), channel_id=1, source_target_pairs={{0,4},{4,0},{8,12},{12,8},{16,20},{20,16},{24,28},{28,24},{1,5},{5... | collective-permute-start | bytes 6291464 | tf_op jit(solution)/shard_map/ppermute | solution.py:52
  77.5 15.5 %collective-permute-start.7 = (bf16[2,128,1536]{2,1,0:T(8,128)(2,1)S(1)}, bf16[2,128,1536]{2,1,0:T(8,128)(2,1)S(1)}, u32[]{:S(2)}, u32[]{:S(2)}) collective-permute-start(bf16[2,128,1536]{2,1,0:T(8,128)(2,1)S(1)} %add_convert_fusion.2.refs_9_.refs_10_), channel_id=1, source_target_pairs={{0,8},{4,20},{8,0},{12,28},{16,24},{20,4},{24,16},{28,12},{1,9},{5... | collective-permute-start | bytes 2359304 | tf_op jit(solution)/shard_map/ppermute | solution.py:49
  92.5 10.8 %collective-permute-start.10 = (bf16[2,256,2048]{2,1,0:T(8,128)(2,1)}, bf16[2,256,2048]{2,1,0:T(8,128)(2,1)S(1)}, u32[]{:S(2)}, u32[]{:S(2)}) collective-permute-start(bf16[2,256,2048]{2,1,0:T(8,128)(2,1)} %get-tuple-element.37), channel_id=1, source_target_pairs={{0,4},{4,0},{8,12},{12,8},{16,20},{20,16},{24,28},{28,24},{1,5},{5... | collective-permute-start | bytes 6291464 | tf_op jit(solution)/shard_map/ppermute | solution.py:52
  93.8 11.2 %collective-permute-start.5 = (bf16[2,64,1024]{2,1,0:T(8,128)(2,1)S(1)}, bf16[2,64,1024]{2,1,0:T(8,128)(2,1)S(1)}, u32[]{:S(2)}, u32[]{:S(2)}) collective-permute-start(bf16[2,64,1024]{2,1,0:T(8,128)(2,1)S(1)} %add_convert_fusion.10.refs_8_), channel_id=1, source_target_pairs={{0,16},{4,12},{8,24},{12,4},{16,0},{20,28},{24,8},{28,20},{1,17},{... | collective-permute-start | bytes 786440 | tf_op jit(solution)/shard_map/ppermute | solution.py:49
  102.7 29.4 %collective-permute-start.11 = (bf16[2,128,2048]{2,1,0:T(8,128)(2,1)S(1)}, bf16[2,128,2048]{2,1,0:T(8,128)(2,1)S(1)}, u32[]{:S(2)}, u32[]{:S(2)}) collective-permute-start(bf16[2,128,2048]{2,1,0:T(8,128)(2,1)S(1)} %add_convert_fusion.1.refs_11_), channel_id=1, source_target_pairs={{0,8},{4,20},{8,0},{12,28},{16,24},{20,4},{24,16},{28,12},{1,9},{5... | collective-permute-start | bytes 3145736 | tf_op jit(solution)/shard_map/ppermute | solution.py:49
  107.0 24.6 %collective-permute-start.16 = (bf16[2,64,2560]{2,1,0:T(8,128)(2,1)S(1)}, bf16[2,64,2560]{2,1,0:T(8,128)(2,1)S(1)}, u32[]{:S(2)}, u32[]{:S(2)}) collective-permute-start(bf16[2,64,2560]{2,1,0:T(8,128)(2,1)S(1)} %get-tuple-element.39.refs_9_.refs_0_), channel_id=1, source_target_pairs={{0,8},{4,20},{8,0},{12,28},{16,24},{20,4},{24,16},{28,12},{1,9},{5... | collective-permute-start | bytes 1966088 | tf_op jit(solution)/shard_map/ppermute | solution.py:49
  108.6 44.5 %collective-permute-start.13 = (bf16[2,128,2048]{2,1,0:T(8,128)(2,1)S(1)}, bf16[2,128,2048]{2,1,0:T(8,128)(2,1)S(1)}, u32[]{:S(2)}, u32[]{:S(2)}) collective-permute-start(bf16[2,128,2048]{2,1,0:T(8,128)(2,1)S(1)} %copy-done.13), channel_id=1, source_target_pairs={{0,8},{4,20},{8,0},{12,28},{16,24},{20,4},{24,16},{28,12},{1,9},{5... | collective-permute-start | bytes 3145736 | tf_op jit(solution)/shard_map/ppermute | solution.py:49
  109.1 26.0 %collective-permute-start.15 = (bf16[2,64,2560]{2,1,0:T(8,128)(2,1)S(1)}, bf16[2,64,2560]{2,1,0:T(8,128)(2,1)S(1)}, u32[]{:S(2)}, u32[]{:S(2)}) collective-permute-start(bf16[2,64,2560]{2,1,0:T(8,128)(2,1)S(1)} %get-tuple-element.39.refs_9_.refs_0_), channel_id=1, source_target_pairs={{0,16},{4,12},{8,24},{12,4},{16,0},{20,28},{24,8},{28,20},{1,17},{... | collective-permute-start | bytes 1966088 | tf_op jit(solution)/shard_map/ppermute | solution.py:49
  131.6 21.5 %collective-permute-start.17 = (bf16[2,64,2560]{2,1,0:T(8,128)(2,1)S(1)}, bf16[2,64,2560]{2,1,0:T(8,128)(2,1)S(1)}, u32[]{:S(2)}, u32[]{:S(2)}) collective-permute-start(bf16[2,64,2560]{2,1,0:T(8,128)(2,1)S(1)} %collective-permute-done.16.refs_2_), channel_id=1, source_target_pairs={{0,16},{4,12},{8,24},{12,4},{16,0},{20,28},{24,8},{28,20},{1,17},{... | collective-permute-start | bytes 1966088 | tf_op jit(solution)/shard_map/ppermute | solution.py:49
  133.5 21.3 %collective-permute-start.12 = (bf16[2,64,2048]{2,1,0:T(8,128)(2,1)S(1)}, bf16[2,64,2048]{2,1,0:T(8,128)(2,1)S(1)}, u32[]{:S(2)}, u32[]{:S(2)}) collective-permute-start(bf16[2,64,2048]{2,1,0:T(8,128)(2,1)S(1)} %add_convert_fusion.4), channel_id=1, source_target_pairs={{0,16},{4,12},{8,24},{12,4},{16,0},{20,28},{24,8},{28,20},{1,17},{... | collective-permute-start | bytes 1572872 | tf_op jit(solution)/shard_map/ppermute | solution.py:49
  135.1 32.0 %collective-permute-start.18 = (bf16[2,64,2560]{2,1,0:T(8,128)(2,1)S(1)}, bf16[2,64,2560]{2,1,0:T(8,128)(2,1)S(1)}, u32[]{:S(2)}, u32[]{:S(2)}) collective-permute-start(bf16[2,64,2560]{2,1,0:T(8,128)(2,1)S(1)} %get-tuple-element.39.refs_9_.refs_0_), channel_id=1, source_target_pairs={{0,4},{4,0},{8,12},{12,8},{16,20},{20,16},{24,28},{28,24},{1,5},{5... | collective-permute-start | bytes 1966088 | tf_op jit(solution)/shard_map/ppermute | solution.py:52
  135.1 33.1 %collective-permute-start.20 = (bf16[2,64,2560]{2,1,0:T(8,128)(2,1)S(1)}, bf16[2,64,2560]{2,1,0:T(8,128)(2,1)S(1)}, u32[]{:S(2)}, u32[]{:S(2)}) collective-permute-start(bf16[2,64,2560]{2,1,0:T(8,128)(2,1)S(1)} %collective-permute-done.16.refs_2_), channel_id=1, source_target_pairs={{0,4},{4,0},{8,12},{12,8},{16,20},{20,16},{24,28},{28,24},{1,5},{5... | collective-permute-start | bytes 1966088 | tf_op jit(solution)/shard_map/ppermute | solution.py:52
  153.1 15.2 %collective-permute-start.19 = (bf16[2,64,2560]{2,1,0:T(8,128)(2,1)S(1)}, bf16[2,64,2560]{2,1,0:T(8,128)(2,1)S(1)}, u32[]{:S(2)}, u32[]{:S(2)}) collective-permute-start(bf16[2,64,2560]{2,1,0:T(8,128)(2,1)S(1)} %collective-permute-done.15.refs_1_), channel_id=1, source_target_pairs={{0,4},{4,0},{8,12},{12,8},{16,20},{20,16},{24,28},{28,24},{1,5},{5... | collective-permute-start | bytes 1966088 | tf_op jit(solution)/shard_map/ppermute | solution.py:52
  153.1 15.2 %collective-permute-start.21 = (bf16[2,64,2560]{2,1,0:T(8,128)(2,1)S(1)}, bf16[2,64,2560]{2,1,0:T(8,128)(2,1)S(1)}, u32[]{:S(2)}, u32[]{:S(2)}) collective-permute-start(bf16[2,64,2560]{2,1,0:T(8,128)(2,1)S(1)} %collective-permute-done.17.refs_3_), channel_id=1, source_target_pairs={{0,4},{4,0},{8,12},{12,8},{16,20},{20,16},{24,28},{28,24},{1,5},{5... | collective-permute-start | bytes 1966088 | tf_op jit(solution)/shard_map/ppermute | solution.py:52
  154.9 9.2 %collective-permute-start.14 = (bf16[2,64,2048]{2,1,0:T(8,128)(2,1)S(1)}, bf16[2,64,2048]{2,1,0:T(8,128)(2,1)S(1)}, u32[]{:S(2)}, u32[]{:S(2)}) collective-permute-start(bf16[2,64,2048]{2,1,0:T(8,128)(2,1)S(1)} %add_convert_fusion.3), channel_id=1, source_target_pairs={{0,16},{4,12},{8,24},{12,4},{16,0},{20,28},{24,8},{28,20},{1,17},{... | collective-permute-start | bytes 1572872 | tf_op jit(solution)/shard_map/ppermute | solution.py:49
  166.8 24.8 %collective-permute-start.23 = (bf16[2,64,4096]{2,1,0:T(8,128)(2,1)S(1)}, bf16[2,64,4096]{2,1,0:T(8,128)(2,1)S(1)}, u32[]{:S(2)}, u32[]{:S(2)}) collective-permute-start(bf16[2,64,4096]{2,1,0:T(8,128)(2,1)S(1)} %get-tuple-element.42.refs_12_.refs_0_), channel_id=1, source_target_pairs={{0,8},{4,20},{8,0},{12,28},{16,24},{20,4},{24,16},{28,12},{1,9},{5... | collective-permute-start | bytes 3145736 | tf_op jit(solution)/shard_map/ppermute | solution.py:49
  167.1 26.4 %collective-permute-start.22 = (bf16[2,64,4096]{2,1,0:T(8,128)(2,1)S(1)}, bf16[2,64,4096]{2,1,0:T(8,128)(2,1)S(1)}, u32[]{:S(2)}, u32[]{:S(2)}) collective-permute-start(bf16[2,64,4096]{2,1,0:T(8,128)(2,1)S(1)} %get-tuple-element.42.refs_12_.refs_0_), channel_id=1, source_target_pairs={{0,16},{4,12},{8,24},{12,4},{16,0},{20,28},{24,8},{28,20},{1,17},{... | collective-permute-start | bytes 3145736 | tf_op jit(solution)/shard_map/ppermute | solution.py:49
  191.6 14.8 %collective-permute-start.24 = (bf16[2,64,4096]{2,1,0:T(8,128)(2,1)S(1)}, bf16[2,64,4096]{2,1,0:T(8,128)(2,1)S(1)}, u32[]{:S(2)}, u32[]{:S(2)}) collective-permute-start(bf16[2,64,4096]{2,1,0:T(8,128)(2,1)S(1)} %collective-permute-done.23.refs_2_), channel_id=1, source_target_pairs={{0,16},{4,12},{8,24},{12,4},{16,0},{20,28},{24,8},{28,20},{1,17},{... | collective-permute-start | bytes 3145736 | tf_op jit(solution)/shard_map/ppermute | solution.py:49
  193.0 13.4 %collective-permute-start.25 = (bf16[2,64,4096]{2,1,0:T(8,128)(2,1)}, bf16[2,64,4096]{2,1,0:T(8,128)(2,1)S(1)}, u32[]{:S(2)}, u32[]{:S(2)}) collective-permute-start(bf16[2,64,4096]{2,1,0:T(8,128)(2,1)} %copy-done), channel_id=1, source_target_pairs={{0,4},{4,0},{8,12},{12,8},{16,20},{20,16},{24,28},{28,24},{1,5},{5... | collective-permute-start | bytes 3145736 | tf_op jit(solution)/shard_map/ppermute | solution.py:52
  193.0 13.4 %collective-permute-start.27 = (bf16[2,64,4096]{2,1,0:T(8,128)(2,1)S(1)}, bf16[2,64,4096]{2,1,0:T(8,128)(2,1)S(1)}, u32[]{:S(2)}, u32[]{:S(2)}) collective-permute-start(bf16[2,64,4096]{2,1,0:T(8,128)(2,1)S(1)} %collective-permute-done.23.refs_2_), channel_id=1, source_target_pairs={{0,4},{4,0},{8,12},{12,8},{16,20},{20,16},{24,28},{28,24},{1,5},{5... | collective-permute-start | bytes 3145736 | tf_op jit(solution)/shard_map/ppermute | solution.py:52
  193.5 12.9 %collective-permute-start.26 = (bf16[2,64,4096]{2,1,0:T(8,128)(2,1)S(1)}, bf16[2,64,4096]{2,1,0:T(8,128)(2,1)S(1)}, u32[]{:S(2)}, u32[]{:S(2)}) collective-permute-start(bf16[2,64,4096]{2,1,0:T(8,128)(2,1)S(1)} %collective-permute-done.22.refs_1_), channel_id=1, source_target_pairs={{0,4},{4,0},{8,12},{12,8},{16,20},{20,16},{24,28},{28,24},{1,5},{5... | collective-permute-start | bytes 3145736 | tf_op jit(solution)/shard_map/ppermute | solution.py:52
  228.3 22.2 %collective-permute-start.29 = (bf16[128,1024]{1,0:T(8,128)(2,1)S(1)}, bf16[128,1024]{1,0:T(8,128)(2,1)S(1)}, u32[]{:S(2)}, u32[]{:S(2)}) collective-permute-start(bf16[128,1024]{1,0:T(8,128)(2,1)S(1)} %get-tuple-element.46), channel_id=1, source_target_pairs={{0,3},{1,2},{2,1},{3,0},{4,7},{5,6},{6,5},{7,4},{8,11},{9,10},{10,... | collective-permute-start | bytes 786440 | tf_op jit(solution)/shard_map/ppermute | solution.py:337
  232.8 22.3 %collective-permute-start.30 = (bf16[128,1024]{1,0:T(8,128)(2,1)S(1)}, bf16[128,1024]{1,0:T(8,128)(2,1)S(1)}, u32[]{:S(2)}, u32[]{:S(2)}) collective-permute-start(bf16[128,1024]{1,0:T(8,128)(2,1)S(1)} %get-tuple-element.47), channel_id=1, source_target_pairs={{0,2},{1,3},{2,0},{3,1},{4,6},{5,7},{6,4},{7,5},{8,10},{9,11},{10,... | collective-permute-start | bytes 786440 | tf_op jit(solution)/shard_map/ppermute | solution.py:337
  232.8 22.3 %collective-permute-start.31 = (bf16[128,1024]{1,0:T(8,128)(2,1)S(1)}, bf16[128,1024]{1,0:T(8,128)(2,1)S(1)}, u32[]{:S(2)}, u32[]{:S(2)}) collective-permute-start(bf16[128,1024]{1,0:T(8,128)(2,1)S(1)} %get-tuple-element.48), channel_id=1, source_target_pairs={{0,1},{1,0},{2,3},{3,2},{4,5},{5,4},{6,7},{7,6},{8,9},{9,8},{10,11... | collective-permute-start | bytes 786440 | tf_op jit(solution)/shard_map/ppermute | solution.py:337
  263.0 13.5 %collective-permute-start.33 = (bf16[128,1024]{1,0:T(8,128)(2,1)S(1)}, bf16[128,1024]{1,0:T(8,128)(2,1)S(1)}, u32[]{:S(2)}, u32[]{:S(2)}) collective-permute-start(bf16[128,1024]{1,0:T(8,128)(2,1)S(1)} %add_convert_fusion.8), channel_id=1, source_target_pairs={{0,2},{1,3},{2,0},{3,1},{4,6},{5,7},{6,4},{7,5},{8,10},{9,11},{10,... | collective-permute-start | bytes 786440 | tf_op jit(solution)/shard_map/ppermute | solution.py:337
  264.2 12.3 %collective-permute-start.34 = (bf16[128,1024]{1,0:T(8,128)(2,1)S(1)}, bf16[128,1024]{1,0:T(8,128)(2,1)S(1)}, u32[]{:S(2)}, u32[]{:S(2)}) collective-permute-start(bf16[128,1024]{1,0:T(8,128)(2,1)S(1)} %get-tuple-element.55), channel_id=1, source_target_pairs={{0,1},{1,0},{2,3},{3,2},{4,5},{5,4},{6,7},{7,6},{8,9},{9,8},{10,11... | collective-permute-start | bytes 786440 | tf_op jit(solution)/shard_map/ppermute | solution.py:337
  (19 other events, 188.5 us)
where the time goes:
time: 278 us
  waiting for transfers between devices  127 us (46%)
  Pallas kernels  103 us (37%)
  starting transfers between devices  31.2 us (11%)
  other arithmetic  9.89 us (4%)
  local copies, waits for them, and re-layouts  5.61 us (2%)
    ppermute x14, waiting for transfers between devices, step(): return lax.ppermute(array, 'row', perm)  70.6 us
    ppermute x9, waiting for transfers between devices, flip(): return lax.ppermute(array, 'col', [(z, z ^ bit) for z in range(size)])  53.4 us
    pallas_call x3, Pallas kernels, backward(): pl.pallas_call(functools.partial(backward_kernel, len(out_shape), tiles,...  52.3 us
    pallas_call x4, Pallas kernels, forward(): pl.pallas_call(functools.partial(forward_kernel, len(xs), len(after)), gr...  46.2 us
    ppermute x9, starting transfers between devices, flip(): return lax.ppermute(array, 'col', [(z, z ^ bit) for z in range(size)])  14.5 us
    ppermute x14, starting transfers between devices, step(): return lax.ppermute(array, 'row', perm)  14 us
    convert_element_type x8, other arithmetic, exchange(): sum((wide(t[:, rows:2 * rows]) for t in self.terms)).astype(jnp.bfloat16)  6.34 us
  transfers between devices with their start and end apart: 35, of which 12 were waited for; matrix products, arithmetic and copies ran while one was open for 4% of the time, Pallas kernels for 28%

commit v1 on v0

--- a/solution.py
+++ b/solution.py
@@ -9,8 +9,8 @@
 from jax.sharding import PartitionSpec as P
 
 BLOCK = 128
-FORWARD = (2, 3, 4, 4)
-BACKWARD = (5, 8)
+FORWARD = (3, 3, 3, 4)
+BACKWARD = (6, 7)
 FEATURE_PARTS = 2
 VMEM_BYTES = 48 * 1024 * 1024
 ANY = pl.BlockSpec(memory_space=pl.ANY)

time: 278 us -> 282 us (1.014)
  starting transfers between devices: 31.2 us -> 35.9 us
    ppermute x14, starting transfers between devices: 14 us -> 18.7 us  [step(): return lax.ppermute(array, 'row', perm)]
  transfers between devices with their start and end apart: 35 -> 35, of which waited for: 12 -> 14; matrix products, arithmetic and copies ran while one was open for 4% -> 4% of each run, Pallas kernels for 28% -> 26%
where the time goes in v1:
time: 282 us; the launch traced here: 281 us
  waiting for transfers between devices  126 us (45%)
  Pallas kernels  102 us (36%)
  starting transfers between devices  35.9 us (13%)
  other arithmetic  9.56 us (3%)
  local copies, waits for them, and re-layouts  5.48 us (2%)
    ppermute x14, waiting for transfers between devices, step(): return lax.ppermute(array, 'row', perm)  67.8 us
    ppermute x9, waiting for transfers between devices, flip(): return lax.ppermute(array, 'col', [(z, z ^ bit) for z in range(size)])  54.7 us
    pallas_call x3, Pallas kernels, backward(): pl.pallas_call(functools.partial(backward_kernel, len(out_shape), tiles,...  52.5 us
    pallas_call x4, Pallas kernels, forward(): pl.pallas_call(functools.partial(forward_kernel, len(xs), len(after)), gr...  45.3 us
    ppermute x14, starting transfers between devices, step(): return lax.ppermute(array, 'row', perm)  18.7 us
    ppermute x9, starting transfers between devices, flip(): return lax.ppermute(array, 'col', [(z, z ^ bit) for z in range(size)])  14.5 us
    convert_element_type x8, other arithmetic, exchange(): sum((wide(t[:, rows:2 * rows]) for t in self.terms)).astype(jnp.bfloat16)  6.02 us
  transfers between devices with their start and end apart: 35, of which 14 were waited for; matrix products, arithmetic and copies ran while one was open for 4% of the time, Pallas kernels for 26%

profile of v1, /device:TPU:0, one launch (start us, length us, event | category | flops | bytes accessed | tf_op | source)
XLA Modules:
  0.0 280.9 jit_solution(7083306390150101341)
XLA Ops:
  0.6 4.1 %collective-permute-start.1 = (bf16[128,2048]{1,0:T(8,128)(2,1)}, bf16[128,2048]{1,0:T(8,128)(2,1)S(1)}, u32[]{:S(2)}, u32[]{:S(2)}) collective-permute-start(bf16[128,2048]{1,0:T(8,128)(2,1)} %refs_0_.7), channel_id=1, source_target_pairs={{0,2},{1,3},{2,0},{3,1},{4,6},{5,7},{6,4},{7,5},{8,10},{9,11},{10,... | collective-permute-start | bytes 1572872 | tf_op jit(solution)/shard_map/ppermute | solution.py:337
  4.7 1.6 collective-permute-start
  6.3 21.9 %collective-permute-done.1.refs_2_ = bf16[128,2048]{1,0:T(8,128)(2,1)S(1)} collective-permute-done((bf16[128,2048]{1,0:T(8,128)(2,1)}, bf16[128,2048]{1,0:T(8,128)(2,1)S(1)}, u32[]{:S(2)}, u32[]{:S(2)}) %collective-permute-start.1) | collective-permute-done | bytes 524320 | tf_op jit(solution)/shard_map/ppermute | solution.py:337
  31.7 9.6 %collective-permute-done.2.refs_3_ = bf16[128,2048]{1,0:T(8,128)(2,1)S(1)} collective-permute-done((bf16[128,2048]{1,0:T(8,128)(2,1)S(1)}, bf16[128,2048]{1,0:T(8,128)(2,1)S(1)}, u32[]{:S(2)}, u32[]{:S(2)}) %collective-permute-start.2) | collective-permute-done | bytes 524320 | tf_op jit(solution)/shard_map/ppermute | solution.py:337
  41.3 10.3 %shard_map.95 = (bf16[2,256,1536]{2,1,0:T(8,128)(2,1)S(1)}, bf16[2,256,1536]{2,1,0:T(8,128)(2,1)S(1)}) custom-call(s32[8]{0:T(128)S(1)} %dynamic-slice_bitcast_fusion.1.slots, bf16[128,2048]{1,0:T(8,128)(2,1)S(1)} %copy-done.4, bf16[128,2048]{1,0:T(8,128)(2,1)S(1)} %collective-permute-done.refs_1_, bf16[128,2048]{1,0:T(8,128)(2,1)S(1)} %collective-permute-done.1.refs_2_, ...), custom_call_target="tpu_custom_call" | custom-call | flops 12884901888 | bytes 12582912 | tf_op jit(solution)/shard_map/pallas_call | solution.py:112
  52.8 10.3 %shard_map.96 = (bf16[2,256,1536]{2,1,0:T(8,128)(2,1)S(1)}, bf16[2,256,1536]{2,1,0:T(8,128)(2,1)S(1)}) custom-call(s32[8]{0:T(128)S(1)} %dynamic-slice_bitcast_fusion.1.slots, bf16[128,2048]{1,0:T(8,128)(2,1)S(1)} %copy-done.4, bf16[128,2048]{1,0:T(8,128)(2,1)S(1)} %collective-permute-done.refs_1_, bf16[128,2048]{1,0:T(8,128)(2,1)S(1)} %collective-permute-done.1.refs_2_, ...), custom_call_target="tpu_custom_call" | custom-call | flops 12884901888 | bytes 12582912 | tf_op jit(solution)/shard_map/pallas_call | solution.py:112
  65.3 1.5 collective-permute-done.6.refs_5_
  67.0 1.3 collective-permute-start.7
  68.3 11.0 %shard_map.97 = (bf16[2,256,1536]{2,1,0:T(8,128)(2,1)S(1)}, bf16[2,256,1536]{2,1,0:T(8,128)(2,1)}) custom-call(s32[8]{0:T(128)S(1)} %dynamic-slice_bitcast_fusion.1.slots, bf16[128,2048]{1,0:T(8,128)(2,1)S(1)} %copy-done.4, bf16[128,2048]{1,0:T(8,128)(2,1)S(1)} %collective-permute-done.refs_1_, bf16[128,2048]{1,0:T(8,128)(2,1)S(1)} %collective-permute-done.1.refs_2_, ...), custom_call_target="tpu_custom_call" | custom-call | flops 12884901888 | bytes 12582912 | tf_op jit(solution)/shard_map/pallas_call | solution.py:112
  79.7 13.6 %shard_map.98 = (bf16[2,256,2048]{2,1,0:T(8,128)(2,1)}, bf16[2,256,2048]{2,1,0:T(8,128)(2,1)}) custom-call(s32[8]{0:T(128)S(1)} %dynamic-slice_bitcast_fusion.1.slots, bf16[128,2048]{1,0:T(8,128)(2,1)S(1)} %copy-done.4, bf16[128,2048]{1,0:T(8,128)(2,1)S(1)} %collective-permute-done.refs_1_, bf16[128,2048]{1,0:T(8,128)(2,1)S(1)} %collective-permute-done.1.refs_2_, ...), custom_call_target="tpu_custom_call" | custom-call | flops 17179869184 | bytes 16777216 | tf_op jit(solution)/shard_map/pallas_call | solution.py:112
  94.9 1.6 collective-permute-start.8
  97.0 5.8 %collective-permute-done.8.refs_7_ = bf16[2,64,1536]{2,1,0:T(8,128)(2,1)S(1)} collective-permute-done((bf16[2,64,1536]{2,1,0:T(8,128)(2,1)S(1)}, bf16[2,64,1536]{2,1,0:T(8,128)(2,1)S(1)}, u32[]{:S(2)}, u32[]{:S(2)}) %collective-permute-start.8) | collective-permute-done | bytes 393248 | tf_op jit(solution)/shard_map/ppermute | solution.py:49
  104.1 1.6 add_convert_fusion.refs_12_
  107.0 2.3 shard_map.99
  113.5 15.4 %collective-permute-done.16.refs_2_ = bf16[2,64,3072]{2,1,0:T(8,128)(2,1)S(1)} collective-permute-done((bf16[2,64,3072]{2,1,0:T(8,128)(2,1)S(1)}, bf16[2,64,3072]{2,1,0:T(8,128)(2,1)S(1)}, u32[]{:S(2)}, u32[]{:S(2)}) %collective-permute-start.16) | collective-permute-done | bytes 786464 | tf_op jit(solution)/shard_map/ppermute | solution.py:49
  128.9 2.4 collective-permute-start.17
  131.3 14.4 %collective-permute-done.11.refs_2_ = bf16[2,128,1536]{2,1,0:T(8,128)(2,1)S(1)} collective-permute-done((bf16[2,128,1536]{2,1,0:T(8,128)(2,1)S(1)}, bf16[2,128,1536]{2,1,0:T(8,128)(2,1)S(1)}, u32[]{:S(2)}, u32[]{:S(2)}) %collective-permute-start.11) | collective-permute-done | bytes 786464 | tf_op jit(solution)/shard_map/ppermute | solution.py:49
  146.9 2.5 collective-permute-start.12
  149.9 12.2 %collective-permute-done.13.refs_6_ = bf16[2,128,2048]{2,1,0:T(8,128)(2,1)S(1)} collective-permute-done((bf16[2,128,2048]{2,1,0:T(8,128)(2,1)S(1)}, bf16[2,128,2048]{2,1,0:T(8,128)(2,1)S(1)}, u32[]{:S(2)}, u32[]{:S(2)}) %collective-permute-start.13) | collective-permute-done | bytes 1048608 | tf_op jit(solution)/shard_map/ppermute | solution.py:49
  162.9 1.6 collective-permute-start.14
  165.2 7.0 %collective-permute-done.14.refs_7_ = bf16[2,64,2048]{2,1,0:T(8,128)(2,1)S(1)} collective-permute-done((bf16[2,64,2048]{2,1,0:T(8,128)(2,1)S(1)}, bf16[2,64,2048]{2,1,0:T(8,128)(2,1)S(1)}, u32[]{:S(2)}, u32[]{:S(2)}) %collective-permute-start.14) | collective-permute-done | bytes 524320 | tf_op jit(solution)/shard_map/ppermute | solution.py:49
  172.2 2.4 shard_map.100
  176.8 21.3 %shard_map.101.refs_12_ = f32[2048,512]{1,0:T(8,128)} custom-call(s32[8]{0:T(128)S(1)} %dynamic-slice_bitcast_fusion.where, bf16[2,64,3072]{2,1,0:T(8,128)(2,1)S(1)} %get-tuple-element.39.refs_9_.refs_0_, bf16[2,64,3072]{2,1,0:T(8,128)(2,1)S(1)} %collective-permute-done.15.refs_1_, bf16[2,64,3072]{2,1,0:T(8,128)(2,1)S(1)} %collective-permute-done.16.refs_2_, ...), custom_call_target="tpu_custom_call" | custom-call | flops 19327352832 | bytes 25165824 | tf_op jit(solution)/shard_map/pallas_call | solution.py:267
  199.8 11.8 %collective-permute-done.24.refs_3_ = bf16[2,64,3584]{2,1,0:T(8,128)(2,1)S(1)} collective-permute-done((bf16[2,64,3584]{2,1,0:T(8,128)(2,1)S(1)}, bf16[2,64,3584]{2,1,0:T(8,128)(2,1)S(1)}, u32[]{:S(2)}, u32[]{:S(2)}) %collective-permute-start.24) | collective-permute-done | bytes 917536 | tf_op jit(solution)/shard_map/ppermute | solution.py:49
  211.6 2.4 collective-permute-done.28.refs_7_
  216.2 15.5 %shard_map.102 = (bf16[128,1024]{1,0:T(8,128)(2,1)S(1)}, bf16[128,1024]{1,0:T(8,128)(2,1)S(1)}, bf16[128,1024]{1,0:T(8,128)(2,1)S(1)}, bf16[128,1024]{1,0:T(8,128)(2,1)S(1)}) custom-call(s32[8]{0:T(128)S(1)} %dynamic-slice_bitcast_fusion.where, bf16[2,64,3584]{2,1,0:T(8,128)(2,1)S(1)} %copy-done.6, bf16[2,64,3584]{2,1,0:T(8,128)(2,1)S(1)} %collective-permute-done.22.refs_1_, ...), custom_call_target="tpu_custom_call" | custom-call | flops 11274289152 | bytes 14680064 | tf_op jit(solution)/shard_map/pallas_call | solution.py:267
  231.7 4.5 %collective-permute-start.29 = (bf16[128,1024]{1,0:T(8,128)(2,1)S(1)}, bf16[128,1024]{1,0:T(8,128)(2,1)S(1)}, u32[]{:S(2)}, u32[]{:S(2)}) collective-permute-start(bf16[128,1024]{1,0:T(8,128)(2,1)S(1)} %get-tuple-element.46), channel_id=1, source_target_pairs={{0,3},{1,2},{2,1},{3,0},{4,7},{5,6},{6,5},{7,4},{8,11},{9,10},{10,... | collective-permute-start | bytes 786440 | tf_op jit(solution)/shard_map/ppermute | solution.py:337
  236.9 15.7 %shard_map.103 = (bf16[128,1024]{1,0:T(8,128)(2,1)S(1)}, bf16[128,1024]{1,0:T(8,128)(2,1)S(1)}, bf16[128,1024]{1,0:T(8,128)(2,1)S(1)}, bf16[128,1024]{1,0:T(8,128)(2,1)S(1)}) custom-call(s32[8]{0:T(128)S(1)} %dynamic-slice_bitcast_fusion.where, bf16[2,64,3584]{2,1,0:T(8,128)(2,1)S(1)} %copy-done.6, bf16[2,64,3584]{2,1,0:T(8,128)(2,1)S(1)} %collective-permute-done.22.refs_1_, ...), custom_call_target="tpu_custom_call" | custom-call | flops 11274289152 | bytes 14680064 | tf_op jit(solution)/shard_map/pallas_call | solution.py:267
  252.6 5.9 %collective-permute-done.30 = bf16[128,1024]{1,0:T(8,128)(2,1)S(1)} collective-permute-done((bf16[128,1024]{1,0:T(8,128)(2,1)S(1)}, bf16[128,1024]{1,0:T(8,128)(2,1)S(1)}, u32[]{:S(2)}, u32[]{:S(2)}) %collective-permute-start.30) | collective-permute-done | bytes 262176 | tf_op jit(solution)/shard_map/ppermute | solution.py:337
  258.6 7.8 %collective-permute-done.32 = bf16[128,1024]{1,0:T(8,128)(2,1)S(1)} collective-permute-done((bf16[128,1024]{1,0:T(8,128)(2,1)S(1)}, bf16[128,1024]{1,0:T(8,128)(2,1)S(1)}, u32[]{:S(2)}, u32[]{:S(2)}) %collective-permute-start.32) | collective-permute-done | bytes 262176 | tf_op jit(solution)/shard_map/ppermute | solution.py:337
  267.7 1.7 collective-permute-start.34
  270.5 9.4 %collective-permute-done.33 = bf16[128,1024]{1,0:T(8,128)(2,1)S(1)} collective-permute-done((bf16[128,1024]{1,0:T(8,128)(2,1)S(1)}, bf16[128,1024]{1,0:T(8,128)(2,1)S(1)}, u32[]{:S(2)}, u32[]{:S(2)}) %collective-permute-start.33) | collective-permute-done | bytes 262176 | tf_op jit(solution)/shard_map/ppermute | solution.py:337
  (102 shorter events, 29.3 us)
Async XLA Ops:
  0.6 27.6 %collective-permute-start.1 = (bf16[128,2048]{1,0:T(8,128)(2,1)}, bf16[128,2048]{1,0:T(8,128)(2,1)S(1)}, u32[]{:S(2)}, u32[]{:S(2)}) collective-permute-start(bf16[128,2048]{1,0:T(8,128)(2,1)} %refs_0_.7), channel_id=1, source_target_pairs={{0,2},{1,3},{2,0},{3,1},{4,6},{5,7},{6,4},{7,5},{8,10},{9,11},{10,... | collective-permute-start | bytes 1572872 | tf_op jit(solution)/shard_map/ppermute | solution.py:337
  4.7 26.9 %collective-permute-start = (bf16[128,2048]{1,0:T(8,128)(2,1)}, bf16[128,2048]{1,0:T(8,128)(2,1)S(1)}, u32[]{:S(2)}, u32[]{:S(2)}) collective-permute-start(bf16[128,2048]{1,0:T(8,128)(2,1)} %refs_0_.7), channel_id=1, source_target_pairs={{0,1},{1,0},{2,3},{3,2},{4,5},{5,4},{6,7},{7,6},{8,9},{9,8},{10,11... | collective-permute-start | bytes 1572872 | tf_op jit(solution)/shard_map/ppermute | solution.py:337
  28.2 13.0 %collective-permute-start.2 = (bf16[128,2048]{1,0:T(8,128)(2,1)S(1)}, bf16[128,2048]{1,0:T(8,128)(2,1)S(1)}, u32[]{:S(2)}, u32[]{:S(2)}) collective-permute-start(bf16[128,2048]{1,0:T(8,128)(2,1)S(1)} %collective-permute-done.1.refs_2_), channel_id=1, source_target_pairs={{0,1},{1,0},{2,3},{3,2},{4,5},{5,4},{6,7},{7,6},{8,9},{9,8},{10,11... | collective-permute-start | bytes 1572872 | tf_op jit(solution)/shard_map/ppermute | solution.py:337
  52.8 10.9 %collective-permute-start.3 = (bf16[2,256,1536]{2,1,0:T(8,128)(2,1)S(1)}, bf16[2,256,1536]{2,1,0:T(8,128)(2,1)S(1)}, u32[]{:S(2)}, u32[]{:S(2)}) collective-permute-start(bf16[2,256,1536]{2,1,0:T(8,128)(2,1)S(1)} %get-tuple-element.30), channel_id=1, source_target_pairs={{0,4},{4,0},{8,12},{12,8},{16,20},{20,16},{24,28},{28,24},{1,5},{5... | collective-permute-start | bytes 4718600 | tf_op jit(solution)/shard_map/ppermute | solution.py:52
  63.9 15.6 %collective-permute-start.4 = (bf16[2,128,1536]{2,1,0:T(8,128)(2,1)S(1)}, bf16[2,128,1536]{2,1,0:T(8,128)(2,1)S(1)}, u32[]{:S(2)}, u32[]{:S(2)}) collective-permute-start(bf16[2,128,1536]{2,1,0:T(8,128)(2,1)S(1)} %add_convert_fusion.3.refs_8_.refs_9_), channel_id=1, source_target_pairs={{0,8},{4,20},{8,0},{12,28},{16,24},{20,4},{24,16},{28,12},{1,9},{5... | collective-permute-start | bytes 2359304 | tf_op jit(solution)/shard_map/ppermute | solution.py:49
  67.0 26.8 %collective-permute-start.7 = (bf16[2,128,1536]{2,1,0:T(8,128)(2,1)S(1)}, bf16[2,128,1536]{2,1,0:T(8,128)(2,1)S(1)}, u32[]{:S(2)}, u32[]{:S(2)}) collective-permute-start(bf16[2,128,1536]{2,1,0:T(8,128)(2,1)S(1)} %add_convert_fusion.2.refs_9_.refs_10_), channel_id=1, source_target_pairs={{0,8},{4,20},{8,0},{12,28},{16,24},{20,4},{24,16},{28,12},{1,9},{5... | collective-permute-start | bytes 2359304 | tf_op jit(solution)/shard_map/ppermute | solution.py:49
  79.3 23.4 %collective-permute-start.9 = (bf16[2,256,1536]{2,1,0:T(8,128)(2,1)}, bf16[2,256,1536]{2,1,0:T(8,128)(2,1)}, u32[]{:S(2)}, u32[]{:S(2)}) collective-permute-start(bf16[2,256,1536]{2,1,0:T(8,128)(2,1)} %get-tuple-element.34), channel_id=1, source_target_pairs={{0,4},{4,0},{8,12},{12,8},{16,20},{20,16},{24,28},{28,24},{1,5},{5... | collective-permute-start | bytes 4718600 | tf_op jit(solution)/shard_map/ppermute | solution.py:52
  93.3 10.8 %collective-permute-start.10 = (bf16[2,256,2048]{2,1,0:T(8,128)(2,1)}, bf16[2,256,2048]{2,1,0:T(8,128)(2,1)S(1)}, u32[]{:S(2)}, u32[]{:S(2)}) collective-permute-start(bf16[2,256,2048]{2,1,0:T(8,128)(2,1)} %get-tuple-element.37), channel_id=1, source_target_pairs={{0,4},{4,0},{8,12},{12,8},{16,20},{20,16},{24,28},{28,24},{1,5},{5... | collective-permute-start | bytes 6291464 | tf_op jit(solution)/shard_map/ppermute | solution.py:52
  94.9 7.8 %collective-permute-start.8 = (bf16[2,64,1536]{2,1,0:T(8,128)(2,1)S(1)}, bf16[2,64,1536]{2,1,0:T(8,128)(2,1)S(1)}, u32[]{:S(2)}, u32[]{:S(2)}) collective-permute-start(bf16[2,64,1536]{2,1,0:T(8,128)(2,1)S(1)} %add_convert_fusion.6), channel_id=1, source_target_pairs={{0,16},{4,12},{8,24},{12,4},{16,0},{20,28},{24,8},{28,20},{1,17},{... | collective-permute-start | bytes 1179656 | tf_op jit(solution)/shard_map/ppermute | solution.py:49
  96.5 10.5 %collective-permute-start.5 = (bf16[2,64,1536]{2,1,0:T(8,128)(2,1)S(1)}, bf16[2,64,1536]{2,1,0:T(8,128)(2,1)S(1)}, u32[]{:S(2)}, u32[]{:S(2)}) collective-permute-start(bf16[2,64,1536]{2,1,0:T(8,128)(2,1)S(1)} %add_convert_fusion.7.refs_8_), channel_id=1, source_target_pairs={{0,16},{4,12},{8,24},{12,4},{16,0},{20,28},{24,8},{28,20},{1,17},{... | collective-permute-start | bytes 1179656 | tf_op jit(solution)/shard_map/ppermute | solution.py:49
  109.3 19.6 %collective-permute-start.16 = (bf16[2,64,3072]{2,1,0:T(8,128)(2,1)S(1)}, bf16[2,64,3072]{2,1,0:T(8,128)(2,1)S(1)}, u32[]{:S(2)}, u32[]{:S(2)}) collective-permute-start(bf16[2,64,3072]{2,1,0:T(8,128)(2,1)S(1)} %get-tuple-element.39.refs_9_.refs_0_), channel_id=1, source_target_pairs={{0,8},{4,20},{8,0},{12,28},{16,24},{20,4},{24,16},{28,12},{1,9},{5... | collective-permute-start | bytes 2359304 | tf_op jit(solution)/shard_map/ppermute | solution.py:49
  110.5 35.2 %collective-permute-start.11 = (bf16[2,128,1536]{2,1,0:T(8,128)(2,1)S(1)}, bf16[2,128,1536]{2,1,0:T(8,128)(2,1)S(1)}, u32[]{:S(2)}, u32[]{:S(2)}) collective-permute-start(bf16[2,128,1536]{2,1,0:T(8,128)(2,1)S(1)} %add_convert_fusion.1.refs_11_), channel_id=1, source_target_pairs={{0,8},{4,20},{8,0},{12,28},{16,24},{20,4},{24,16},{28,12},{1,9},{5... | collective-permute-start | bytes 2359304 | tf_op jit(solution)/shard_map/ppermute | solution.py:49
  111.4 50.7 %collective-permute-start.13 = (bf16[2,128,2048]{2,1,0:T(8,128)(2,1)S(1)}, bf16[2,128,2048]{2,1,0:T(8,128)(2,1)S(1)}, u32[]{:S(2)}, u32[]{:S(2)}) collective-permute-start(bf16[2,128,2048]{2,1,0:T(8,128)(2,1)S(1)} %copy-done.13), channel_id=1, source_target_pairs={{0,8},{4,20},{8,0},{12,28},{16,24},{20,4},{24,16},{28,12},{1,9},{5... | collective-permute-start | bytes 3145736 | tf_op jit(solution)/shard_map/ppermute | solution.py:49
  112.6 36.8 %collective-permute-start.15 = (bf16[2,64,3072]{2,1,0:T(8,128)(2,1)S(1)}, bf16[2,64,3072]{2,1,0:T(8,128)(2,1)S(1)}, u32[]{:S(2)}, u32[]{:S(2)}) collective-permute-start(bf16[2,64,3072]{2,1,0:T(8,128)(2,1)S(1)} %get-tuple-element.39.refs_9_.refs_0_), channel_id=1, source_target_pairs={{0,16},{4,12},{8,24},{12,4},{16,0},{20,28},{24,8},{28,20},{1,17},{... | collective-permute-start | bytes 2359304 | tf_op jit(solution)/shard_map/ppermute | solution.py:49
  128.9 33.2 %collective-permute-start.17 = (bf16[2,64,3072]{2,1,0:T(8,128)(2,1)S(1)}, bf16[2,64,3072]{2,1,0:T(8,128)(2,1)S(1)}, u32[]{:S(2)}, u32[]{:S(2)}) collective-permute-start(bf16[2,64,3072]{2,1,0:T(8,128)(2,1)S(1)} %collective-permute-done.16.refs_2_), channel_id=1, source_target_pairs={{0,16},{4,12},{8,24},{12,4},{16,0},{20,28},{24,8},{28,20},{1,17},{... | collective-permute-start | bytes 2359304 | tf_op jit(solution)/shard_map/ppermute | solution.py:49
  146.9 16.0 %collective-permute-start.12 = (bf16[2,64,1536]{2,1,0:T(8,128)(2,1)S(1)}, bf16[2,64,1536]{2,1,0:T(8,128)(2,1)S(1)}, u32[]{:S(2)}, u32[]{:S(2)}) collective-permute-start(bf16[2,64,1536]{2,1,0:T(8,128)(2,1)S(1)} %add_convert_fusion.5), channel_id=1, source_target_pairs={{0,16},{4,12},{8,24},{12,4},{16,0},{20,28},{24,8},{28,20},{1,17},{... | collective-permute-start | bytes 1179656 | tf_op jit(solution)/shard_map/ppermute | solution.py:49
  149.4 26.4 %collective-permute-start.18 = (bf16[2,64,3072]{2,1,0:T(8,128)(2,1)S(1)}, bf16[2,64,3072]{2,1,0:T(8,128)(2,1)S(1)}, u32[]{:S(2)}, u32[]{:S(2)}) collective-permute-start(bf16[2,64,3072]{2,1,0:T(8,128)(2,1)S(1)} %get-tuple-element.39.refs_9_.refs_0_), channel_id=1, source_target_pairs={{0,4},{4,0},{8,12},{12,8},{16,20},{20,16},{24,28},{28,24},{1,5},{5... | collective-permute-start | bytes 2359304 | tf_op jit(solution)/shard_map/ppermute | solution.py:52
  149.4 27.3 %collective-permute-start.20 = (bf16[2,64,3072]{2,1,0:T(8,128)(2,1)S(1)}, bf16[2,64,3072]{2,1,0:T(8,128)(2,1)S(1)}, u32[]{:S(2)}, u32[]{:S(2)}) collective-permute-start(bf16[2,64,3072]{2,1,0:T(8,128)(2,1)S(1)} %collective-permute-done.16.refs_2_), channel_id=1, source_target_pairs={{0,4},{4,0},{8,12},{12,8},{16,20},{20,16},{24,28},{28,24},{1,5},{5... | collective-permute-start | bytes 2359304 | tf_op jit(solution)/shard_map/ppermute | solution.py:52
  162.1 14.6 %collective-permute-start.19 = (bf16[2,64,3072]{2,1,0:T(8,128)(2,1)S(1)}, bf16[2,64,3072]{2,1,0:T(8,128)(2,1)S(1)}, u32[]{:S(2)}, u32[]{:S(2)}) collective-permute-start(bf16[2,64,3072]{2,1,0:T(8,128)(2,1)S(1)} %collective-permute-done.15.refs_1_), channel_id=1, source_target_pairs={{0,4},{4,0},{8,12},{12,8},{16,20},{20,16},{24,28},{28,24},{1,5},{5... | collective-permute-start | bytes 2359304 | tf_op jit(solution)/shard_map/ppermute | solution.py:52
  162.1 14.6 %collective-permute-start.21 = (bf16[2,64,3072]{2,1,0:T(8,128)(2,1)S(1)}, bf16[2,64,3072]{2,1,0:T(8,128)(2,1)}, u32[]{:S(2)}, u32[]{:S(2)}) collective-permute-start(bf16[2,64,3072]{2,1,0:T(8,128)(2,1)S(1)} %collective-permute-done.17.refs_3_), channel_id=1, source_target_pairs={{0,4},{4,0},{8,12},{12,8},{16,20},{20,16},{24,28},{28,24},{1,5},{5... | collective-permute-start | bytes 2359304 | tf_op jit(solution)/shard_map/ppermute | solution.py:52
  162.9 9.2 %collective-permute-start.14 = (bf16[2,64,2048]{2,1,0:T(8,128)(2,1)S(1)}, bf16[2,64,2048]{2,1,0:T(8,128)(2,1)S(1)}, u32[]{:S(2)}, u32[]{:S(2)}) collective-permute-start(bf16[2,64,2048]{2,1,0:T(8,128)(2,1)S(1)} %add_convert_fusion.4), channel_id=1, source_target_pairs={{0,16},{4,12},{8,24},{12,4},{16,0},{20,28},{24,8},{28,20},{1,17},{... | collective-permute-start | bytes 1572872 | tf_op jit(solution)/shard_map/ppermute | solution.py:49
  174.6 23.4 %collective-permute-start.23 = (bf16[2,64,3584]{2,1,0:T(8,128)(2,1)S(1)}, bf16[2,64,3584]{2,1,0:T(8,128)(2,1)S(1)}, u32[]{:S(2)}, u32[]{:S(2)}) collective-permute-start(bf16[2,64,3584]{2,1,0:T(8,128)(2,1)S(1)} %get-tuple-element.42.refs_12_.refs_0_), channel_id=1, source_target_pairs={{0,8},{4,20},{8,0},{12,28},{16,24},{20,4},{24,16},{28,12},{1,9},{5... | collective-permute-start | bytes 2752520 | tf_op jit(solution)/shard_map/ppermute | solution.py:49
  175.8 23.9 %collective-permute-start.22 = (bf16[2,64,3584]{2,1,0:T(8,128)(2,1)S(1)}, bf16[2,64,3584]{2,1,0:T(8,128)(2,1)S(1)}, u32[]{:S(2)}, u32[]{:S(2)}) collective-permute-start(bf16[2,64,3584]{2,1,0:T(8,128)(2,1)S(1)} %get-tuple-element.42.refs_12_.refs_0_), channel_id=1, source_target_pairs={{0,16},{4,12},{8,24},{12,4},{16,0},{20,28},{24,8},{28,20},{1,17},{... | collective-permute-start | bytes 2752520 | tf_op jit(solution)/shard_map/ppermute | solution.py:49
  198.1 13.5 %collective-permute-start.24 = (bf16[2,64,3584]{2,1,0:T(8,128)(2,1)S(1)}, bf16[2,64,3584]{2,1,0:T(8,128)(2,1)S(1)}, u32[]{:S(2)}, u32[]{:S(2)}) collective-permute-start(bf16[2,64,3584]{2,1,0:T(8,128)(2,1)S(1)} %collective-permute-done.23.refs_2_), channel_id=1, source_target_pairs={{0,16},{4,12},{8,24},{12,4},{16,0},{20,28},{24,8},{28,20},{1,17},{... | collective-permute-start | bytes 2752520 | tf_op jit(solution)/shard_map/ppermute | solution.py:49
  199.2 12.3 %collective-permute-start.25 = (bf16[2,64,3584]{2,1,0:T(8,128)(2,1)}, bf16[2,64,3584]{2,1,0:T(8,128)(2,1)S(1)}, u32[]{:S(2)}, u32[]{:S(2)}) collective-permute-start(bf16[2,64,3584]{2,1,0:T(8,128)(2,1)} %copy-done.5), channel_id=1, source_target_pairs={{0,4},{4,0},{8,12},{12,8},{16,20},{20,16},{24,28},{28,24},{1,5},{5... | collective-permute-start | bytes 2752520 | tf_op jit(solution)/shard_map/ppermute | solution.py:52
  199.2 12.3 %collective-permute-start.27 = (bf16[2,64,3584]{2,1,0:T(8,128)(2,1)S(1)}, bf16[2,64,3584]{2,1,0:T(8,128)(2,1)S(1)}, u32[]{:S(2)}, u32[]{:S(2)}) collective-permute-start(bf16[2,64,3584]{2,1,0:T(8,128)(2,1)S(1)} %collective-permute-done.23.refs_2_), channel_id=1, source_target_pairs={{0,4},{4,0},{8,12},{12,8},{16,20},{20,16},{24,28},{28,24},{1,5},{5... | collective-permute-start | bytes 2752520 | tf_op jit(solution)/shard_map/ppermute | solution.py:52
  199.7 11.8 %collective-permute-start.26 = (bf16[2,64,3584]{2,1,0:T(8,128)(2,1)S(1)}, bf16[2,64,3584]{2,1,0:T(8,128)(2,1)S(1)}, u32[]{:S(2)}, u32[]{:S(2)}) collective-permute-start(bf16[2,64,3584]{2,1,0:T(8,128)(2,1)S(1)} %collective-permute-done.22.refs_1_), channel_id=1, source_target_pairs={{0,4},{4,0},{8,12},{12,8},{16,20},{20,16},{24,28},{28,24},{1,5},{5... | collective-permute-start | bytes 2752520 | tf_op jit(solution)/shard_map/ppermute | solution.py:52
  231.7 20.9 %collective-permute-start.29 = (bf16[128,1024]{1,0:T(8,128)(2,1)S(1)}, bf16[128,1024]{1,0:T(8,128)(2,1)S(1)}, u32[]{:S(2)}, u32[]{:S(2)}) collective-permute-start(bf16[128,1024]{1,0:T(8,128)(2,1)S(1)} %get-tuple-element.46), channel_id=1, source_target_pairs={{0,3},{1,2},{2,1},{3,0},{4,7},{5,6},{6,5},{7,4},{8,11},{9,10},{10,... | collective-permute-start | bytes 786440 | tf_op jit(solution)/shard_map/ppermute | solution.py:337
  236.3 22.3 %collective-permute-start.30 = (bf16[128,1024]{1,0:T(8,128)(2,1)S(1)}, bf16[128,1024]{1,0:T(8,128)(2,1)S(1)}, u32[]{:S(2)}, u32[]{:S(2)}) collective-permute-start(bf16[128,1024]{1,0:T(8,128)(2,1)S(1)} %get-tuple-element.47), channel_id=1, source_target_pairs={{0,2},{1,3},{2,0},{3,1},{4,6},{5,7},{6,4},{7,5},{8,10},{9,11},{10,... | collective-permute-start | bytes 786440 | tf_op jit(solution)/shard_map/ppermute | solution.py:337
  236.3 22.3 %collective-permute-start.31 = (bf16[128,1024]{1,0:T(8,128)(2,1)S(1)}, bf16[128,1024]{1,0:T(8,128)(2,1)S(1)}, u32[]{:S(2)}, u32[]{:S(2)}) collective-permute-start(bf16[128,1024]{1,0:T(8,128)(2,1)S(1)} %get-tuple-element.48), channel_id=1, source_target_pairs={{0,1},{1,0},{2,3},{3,2},{4,5},{5,4},{6,7},{7,6},{8,9},{9,8},{10,11... | collective-permute-start | bytes 786440 | tf_op jit(solution)/shard_map/ppermute | solution.py:337
  266.5 13.5 %collective-permute-start.33 = (bf16[128,1024]{1,0:T(8,128)(2,1)S(1)}, bf16[128,1024]{1,0:T(8,128)(2,1)S(1)}, u32[]{:S(2)}, u32[]{:S(2)}) collective-permute-start(bf16[128,1024]{1,0:T(8,128)(2,1)S(1)} %add_convert_fusion.9), channel_id=1, source_target_pairs={{0,2},{1,3},{2,0},{3,1},{4,6},{5,7},{6,4},{7,5},{8,10},{9,11},{10,... | collective-permute-start | bytes 786440 | tf_op jit(solution)/shard_map/ppermute | solution.py:337
  267.7 12.3 %collective-permute-start.34 = (bf16[128,1024]{1,0:T(8,128)(2,1)S(1)}, bf16[128,1024]{1,0:T(8,128)(2,1)S(1)}, u32[]{:S(2)}, u32[]{:S(2)}) collective-permute-start(bf16[128,1024]{1,0:T(8,128)(2,1)S(1)} %get-tuple-element.55), channel_id=1, source_target_pairs={{0,1},{1,0},{2,3},{3,2},{4,5},{5,4},{6,7},{7,6},{8,9},{9,8},{10,11... | collective-permute-start | bytes 786440 | tf_op jit(solution)/shard_map/ppermute | solution.py:337
  (20 other events, 345.5 us)

commit v2 on v0

--- a/solution.py
+++ b/solution.py
@@ -12,7 +12,7 @@
 FORWARD = (2, 3, 4, 4)
 BACKWARD = (5, 8)
 FEATURE_PARTS = 2
-VMEM_BYTES = 48 * 1024 * 1024
+VMEM_BYTES = 36 * 1024 * 1024
 ANY = pl.BlockSpec(memory_space=pl.ANY)
 COST = pl.CostEstimate(flops=1, bytes_accessed=1, transcendentals=0)
 

time: 278 us -> 268 us (0.964)
  Pallas kernels: 103 us -> 92 us
  waiting for transfers between devices: 127 us -> 136 us
  other arithmetic: 9.89 us -> 5.44 us
    ppermute x14, waiting for transfers between devices: 70.6 us -> 77.7 us  [step(): return lax.ppermute(array, 'row', perm)]
    pallas_call x3, Pallas kernels: 52.3 us -> 45.7 us  [backward(): pl.pallas_call(functools.partial(backward_kernel, len(out_shape), tiles,...]
    convert_element_type x8, other arithmetic: 6.34 us -> 1.9 us  [exchange(): sum((wide(t[:, rows:2 * rows]) for t in self.terms)).astype(jnp.bfloat16)]
  transfers between devices with their start and end apart: 35 -> 35, of which waited for: 12 -> 14; matrix products, arithmetic and copies ran while one was open for 4% -> 2% of each run, Pallas kernels for 28% -> 26%
where the time goes in v2:
time: 268 us
  waiting for transfers between devices  136 us (51%)
  Pallas kernels  92 us (34%)
  starting transfers between devices  30.2 us (11%)
  other arithmetic  5.44 us (2%)
  local copies, waits for them, and re-layouts  3.04 us (1%)
    ppermute x14, waiting for transfers between devices, step(): return lax.ppermute(array, 'row', perm)  77.7 us
    ppermute x9, waiting for transfers between devices, flip(): return lax.ppermute(array, 'col', [(z, z ^ bit) for z in range(size)])  55.8 us
    pallas_call x3, Pallas kernels, backward(): pl.pallas_call(functools.partial(backward_kernel, len(out_shape), tiles,...  45.7 us
    pallas_call x4, Pallas kernels, forward(): pl.pallas_call(functools.partial(forward_kernel, len(xs), len(after)), gr...  43.8 us
    ppermute x9, starting transfers between devices, flip(): return lax.ppermute(array, 'col', [(z, z ^ bit) for z in range(size)])  14.5 us
    ppermute x14, starting transfers between devices, step(): return lax.ppermute(array, 'row', perm)  13 us
  transfers between devices with their start and end apart: 35, of which 14 were waited for; matrix products, arithmetic and copies ran while one was open for 2% of the time, Pallas kernels for 26%

profile of v2, /device:TPU:0, one launch (start us, length us, event | category | flops | bytes accessed | tf_op | source)
XLA Modules:
  0.0 267.8 jit_solution(8242617348570851299)
XLA Ops:
  0.6 4.1 %collective-permute-start.1 = (bf16[128,2048]{1,0:T(8,128)(2,1)}, bf16[128,2048]{1,0:T(8,128)(2,1)S(1)}, u32[]{:S(2)}, u32[]{:S(2)}) collective-permute-start(bf16[128,2048]{1,0:T(8,128)(2,1)} %refs_0_.7), channel_id=1, source_target_pairs={{0,2},{1,3},{2,0},{3,1},{4,6},{5,7},{6,4},{7,5},{8,10},{9,11},{10,... | collective-permute-start | bytes 1572872 | tf_op jit(solution)/shard_map/ppermute | solution.py:337
  4.7 1.6 collective-permute-start
  6.3 21.9 %collective-permute-done.1.refs_2_ = bf16[128,2048]{1,0:T(8,128)(2,1)S(1)} collective-permute-done((bf16[128,2048]{1,0:T(8,128)(2,1)}, bf16[128,2048]{1,0:T(8,128)(2,1)S(1)}, u32[]{:S(2)}, u32[]{:S(2)}) %collective-permute-start.1) | collective-permute-done | bytes 524320 | tf_op jit(solution)/shard_map/ppermute | solution.py:337
  31.7 9.6 %collective-permute-done.2.refs_3_ = bf16[128,2048]{1,0:T(8,128)(2,1)S(1)} collective-permute-done((bf16[128,2048]{1,0:T(8,128)(2,1)S(1)}, bf16[128,2048]{1,0:T(8,128)(2,1)S(1)}, u32[]{:S(2)}, u32[]{:S(2)}) %collective-permute-start.2) | collective-permute-done | bytes 524320 | tf_op jit(solution)/shard_map/ppermute | solution.py:337
  42.3 7.9 %shard_map.95 = (bf16[2,256,1024]{2,1,0:T(8,128)(2,1)S(1)}, bf16[2,256,1024]{2,1,0:T(8,128)(2,1)S(1)}) custom-call(s32[8]{0:T(128)S(1)} %dynamic-slice_bitcast_fusion.1.slots, bf16[128,2048]{1,0:T(8,128)(2,1)S(1)} %copy-done.1, bf16[128,2048]{1,0:T(8,128)(2,1)S(1)} %collective-permute-done.refs_1_, bf16[128,2048]{1,0:T(8,128)(2,1)S(1)} %collective-permute-done.1.refs_2_, ...), custom_call_target="tpu_custom_call" | custom-call | flops 8589934592 | bytes 8388608 | tf_op jit(solution)/shard_map/pallas_call | solution.py:112
  50.3 10.3 %shard_map.96 = (bf16[2,256,1536]{2,1,0:T(8,128)(2,1)S(1)}, bf16[2,256,1536]{2,1,0:T(8,128)(2,1)S(1)}) custom-call(s32[8]{0:T(128)S(1)} %dynamic-slice_bitcast_fusion.1.slots, bf16[128,2048]{1,0:T(8,128)(2,1)S(1)} %copy-done.1, bf16[128,2048]{1,0:T(8,128)(2,1)S(1)} %collective-permute-done.refs_1_, bf16[128,2048]{1,0:T(8,128)(2,1)S(1)} %collective-permute-done.1.refs_2_, ...), custom_call_target="tpu_custom_call" | custom-call | flops 12884901888 | bytes 12582912 | tf_op jit(solution)/shard_map/pallas_call | solution.py:112
  61.4 1.3 collective-permute-start.4
  62.7 12.8 %shard_map.97 = (bf16[2,256,2048]{2,1,0:T(8,128)(2,1)S(1)}, bf16[2,256,2048]{2,1,0:T(8,128)(2,1)S(1)}) custom-call(s32[8]{0:T(128)S(1)} %dynamic-slice_bitcast_fusion.1.slots, bf16[128,2048]{1,0:T(8,128)(2,1)S(1)} %copy-done.1, bf16[128,2048]{1,0:T(8,128)(2,1)S(1)} %collective-permute-done.refs_1_, bf16[128,2048]{1,0:T(8,128)(2,1)S(1)} %collective-permute-done.1.refs_2_, ...), custom_call_target="tpu_custom_call" | custom-call | flops 17179869184 | bytes 16777216 | tf_op jit(solution)/shard_map/pallas_call | solution.py:112
  75.8 1.3 collective-permute-start.7
  77.2 12.8 %shard_map.98 = (bf16[2,256,2048]{2,1,0:T(8,128)(2,1)S(1)}, bf16[2,256,2048]{2,1,0:T(8,128)(2,1)S(1)}) custom-call(s32[8]{0:T(128)S(1)} %dynamic-slice_bitcast_fusion.1.slots, bf16[128,2048]{1,0:T(8,128)(2,1)S(1)} %copy-done.1, bf16[128,2048]{1,0:T(8,128)(2,1)S(1)} %collective-permute-done.refs_1_, bf16[128,2048]{1,0:T(8,128)(2,1)S(1)} %collective-permute-done.1.refs_2_, ...), custom_call_target="tpu_custom_call" | custom-call | flops 17179869184 | bytes 16777216 | tf_op jit(solution)/shard_map/pallas_call | solution.py:112
  91.3 1.5 collective-permute-start.5
  92.8 5.8 %collective-permute-done.8.refs_7_ = bf16[2,64,1536]{2,1,0:T(8,128)(2,1)S(1)} collective-permute-done((bf16[2,64,1536]{2,1,0:T(8,128)(2,1)S(1)}, bf16[2,64,1536]{2,1,0:T(8,128)(2,1)S(1)}, u32[]{:S(2)}, u32[]{:S(2)}) %collective-permute-start.8) | collective-permute-done | bytes 393248 | tf_op jit(solution)/shard_map/ppermute | solution.py:49
  100.0 1.9 collective-permute-done.5.refs_3_
  103.3 1.8 collective-permute-start.13
  105.3 22.6 %collective-permute-done.16.refs_2_ = bf16[2,64,2560]{2,1,0:T(8,128)(2,1)S(1)} collective-permute-done((bf16[2,64,2560]{2,1,0:T(8,128)(2,1)S(1)}, bf16[2,64,2560]{2,1,0:T(8,128)(2,1)S(1)}, u32[]{:S(2)}, u32[]{:S(2)}) %collective-permute-start.16) | collective-permute-done | bytes 655392 | tf_op jit(solution)/shard_map/ppermute | solution.py:49
  128.6 1.6 collective-permute-start.12
  130.7 18.1 %collective-permute-done.13.refs_6_ = bf16[2,128,2048]{2,1,0:T(8,128)(2,1)S(1)} collective-permute-done((bf16[2,128,2048]{2,1,0:T(8,128)(2,1)S(1)}, bf16[2,128,2048]{2,1,0:T(8,128)(2,1)S(1)}, u32[]{:S(2)}, u32[]{:S(2)}) %collective-permute-start.13) | collective-permute-done | bytes 1048608 | tf_op jit(solution)/shard_map/ppermute | solution.py:49
  151.7 8.0 %collective-permute-done.14.refs_7_ = bf16[2,64,2048]{2,1,0:T(8,128)(2,1)S(1)} collective-permute-done((bf16[2,64,2048]{2,1,0:T(8,128)(2,1)S(1)}, bf16[2,64,2048]{2,1,0:T(8,128)(2,1)S(1)}, u32[]{:S(2)}, u32[]{:S(2)}) %collective-permute-start.14) | collective-permute-done | bytes 524320 | tf_op jit(solution)/shard_map/ppermute | solution.py:49
  159.7 1.5 shard_map.100
  161.8 1.3 collective-permute-start.22
  163.1 16.6 %shard_map.101.refs_12_ = f32[2048,512]{1,0:T(8,128)S(1)} custom-call(s32[8]{0:T(128)S(1)} %dynamic-slice_bitcast_fusion.where, bf16[2,64,2560]{2,1,0:T(8,128)(2,1)S(1)} %get-tuple-element.39.refs_9_.refs_0_, bf16[2,64,2560]{2,1,0:T(8,128)(2,1)S(1)} %collective-permute-done.15.refs_1_, bf16[2,64,2560]{2,1,0:T(8,128)(2,1)S(1)} %collective-permute-done.16.refs_2_, ...), custom_call_target="tpu_custom_call" | custom-call | flops 16106127360 | bytes 20971520 | tf_op jit(solution)/shard_map/pallas_call | solution.py:267
  179.7 7.0 %collective-permute-done.23.refs_2_ = bf16[2,64,4096]{2,1,0:T(8,128)(2,1)S(1)} collective-permute-done((bf16[2,64,4096]{2,1,0:T(8,128)(2,1)S(1)}, bf16[2,64,4096]{2,1,0:T(8,128)(2,1)S(1)}, u32[]{:S(2)}, u32[]{:S(2)}) %collective-permute-start.23) | collective-permute-done | bytes 1048608 | tf_op jit(solution)/shard_map/ppermute | solution.py:49
  188.0 13.5 %collective-permute-done.24.refs_3_ = bf16[2,64,4096]{2,1,0:T(8,128)(2,1)S(1)} collective-permute-done((bf16[2,64,4096]{2,1,0:T(8,128)(2,1)S(1)}, bf16[2,64,4096]{2,1,0:T(8,128)(2,1)S(1)}, u32[]{:S(2)}, u32[]{:S(2)}) %collective-permute-start.24) | collective-permute-done | bytes 1048608 | tf_op jit(solution)/shard_map/ppermute | solution.py:49
  201.5 2.6 collective-permute-done.28.refs_7_
  204.1 14.6 %shard_map.102 = (bf16[128,1024]{1,0:T(8,128)(2,1)S(1)}, bf16[128,1024]{1,0:T(8,128)(2,1)S(1)}, bf16[128,1024]{1,0:T(8,128)(2,1)S(1)}, bf16[128,1024]{1,0:T(8,128)(2,1)S(1)}) custom-call(s32[8]{0:T(128)S(1)} %dynamic-slice_bitcast_fusion.where, bf16[2,64,4096]{2,1,0:T(8,128)(2,1)S(1)} %get-tuple-element.42.refs_12_.refs_0_, ...), custom_call_target="tpu_custom_call" | custom-call | flops 12884901888 | bytes 16777216 | tf_op jit(solution)/shard_map/pallas_call | solution.py:267
  218.7 4.5 %collective-permute-start.29 = (bf16[128,1024]{1,0:T(8,128)(2,1)S(1)}, bf16[128,1024]{1,0:T(8,128)(2,1)S(1)}, u32[]{:S(2)}, u32[]{:S(2)}) collective-permute-start(bf16[128,1024]{1,0:T(8,128)(2,1)S(1)} %get-tuple-element.46), channel_id=1, source_target_pairs={{0,3},{1,2},{2,1},{3,0},{4,7},{5,6},{6,5},{7,4},{8,11},{9,10},{10,... | collective-permute-start | bytes 786440 | tf_op jit(solution)/shard_map/ppermute | solution.py:337
  223.8 14.6 %shard_map.103 = (bf16[128,1024]{1,0:T(8,128)(2,1)S(1)}, bf16[128,1024]{1,0:T(8,128)(2,1)S(1)}, bf16[128,1024]{1,0:T(8,128)(2,1)S(1)}, bf16[128,1024]{1,0:T(8,128)(2,1)S(1)}) custom-call(s32[8]{0:T(128)S(1)} %dynamic-slice_bitcast_fusion.where, bf16[2,64,4096]{2,1,0:T(8,128)(2,1)S(1)} %get-tuple-element.42.refs_12_.refs_0_, ...), custom_call_target="tpu_custom_call" | custom-call | flops 12884901888 | bytes 16777216 | tf_op jit(solution)/shard_map/pallas_call | solution.py:267
  238.4 7.1 %collective-permute-done.30 = bf16[128,1024]{1,0:T(8,128)(2,1)S(1)} collective-permute-done((bf16[128,1024]{1,0:T(8,128)(2,1)S(1)}, bf16[128,1024]{1,0:T(8,128)(2,1)S(1)}, u32[]{:S(2)}, u32[]{:S(2)}) %collective-permute-start.30) | collective-permute-done | bytes 262176 | tf_op jit(solution)/shard_map/ppermute | solution.py:337
  245.5 7.8 %collective-permute-done.32 = bf16[128,1024]{1,0:T(8,128)(2,1)S(1)} collective-permute-done((bf16[128,1024]{1,0:T(8,128)(2,1)S(1)}, bf16[128,1024]{1,0:T(8,128)(2,1)S(1)}, u32[]{:S(2)}, u32[]{:S(2)}) %collective-permute-start.32) | collective-permute-done | bytes 262176 | tf_op jit(solution)/shard_map/ppermute | solution.py:337
  253.4 1.2 collective-permute-start.33
  254.6 1.7 collective-permute-start.34
  257.4 9.4 %collective-permute-done.33 = bf16[128,1024]{1,0:T(8,128)(2,1)S(1)} collective-permute-done((bf16[128,1024]{1,0:T(8,128)(2,1)S(1)}, bf16[128,1024]{1,0:T(8,128)(2,1)S(1)}, u32[]{:S(2)}, u32[]{:S(2)}) %collective-permute-start.33) | collective-permute-done | bytes 262176 | tf_op jit(solution)/shard_map/ppermute | solution.py:337
  (76 shorter events, 18.9 us)
Async XLA Ops:
  0.6 27.6 %collective-permute-start.1 = (bf16[128,2048]{1,0:T(8,128)(2,1)}, bf16[128,2048]{1,0:T(8,128)(2,1)S(1)}, u32[]{:S(2)}, u32[]{:S(2)}) collective-permute-start(bf16[128,2048]{1,0:T(8,128)(2,1)} %refs_0_.7), channel_id=1, source_target_pairs={{0,2},{1,3},{2,0},{3,1},{4,6},{5,7},{6,4},{7,5},{8,10},{9,11},{10,... | collective-permute-start | bytes 1572872 | tf_op jit(solution)/shard_map/ppermute | solution.py:337
  4.7 26.9 %collective-permute-start = (bf16[128,2048]{1,0:T(8,128)(2,1)}, bf16[128,2048]{1,0:T(8,128)(2,1)S(1)}, u32[]{:S(2)}, u32[]{:S(2)}) collective-permute-start(bf16[128,2048]{1,0:T(8,128)(2,1)} %refs_0_.7), channel_id=1, source_target_pairs={{0,1},{1,0},{2,3},{3,2},{4,5},{5,4},{6,7},{7,6},{8,9},{9,8},{10,11... | collective-permute-start | bytes 1572872 | tf_op jit(solution)/shard_map/ppermute | solution.py:337
  28.2 13.0 %collective-permute-start.2 = (bf16[128,2048]{1,0:T(8,128)(2,1)S(1)}, bf16[128,2048]{1,0:T(8,128)(2,1)S(1)}, u32[]{:S(2)}, u32[]{:S(2)}) collective-permute-start(bf16[128,2048]{1,0:T(8,128)(2,1)S(1)} %collective-permute-done.1.refs_2_), channel_id=1, source_target_pairs={{0,1},{1,0},{2,3},{3,2},{4,5},{5,4},{6,7},{7,6},{8,9},{9,8},{10,11... | collective-permute-start | bytes 1572872 | tf_op jit(solution)/shard_map/ppermute | solution.py:337
  50.2 11.0 %collective-permute-start.3 = (bf16[2,256,1024]{2,1,0:T(8,128)(2,1)S(1)}, bf16[2,256,1024]{2,1,0:T(8,128)(2,1)S(1)}, u32[]{:S(2)}, u32[]{:S(2)}) collective-permute-start(bf16[2,256,1024]{2,1,0:T(8,128)(2,1)S(1)} %get-tuple-element.30), channel_id=1, source_target_pairs={{0,4},{4,0},{8,12},{12,8},{16,20},{20,16},{24,28},{28,24},{1,5},{5... | collective-permute-start | bytes 3145736 | tf_op jit(solution)/shard_map/ppermute | solution.py:52
  60.6 15.0 %collective-permute-start.6 = (bf16[2,256,1536]{2,1,0:T(8,128)(2,1)S(1)}, bf16[2,256,1536]{2,1,0:T(8,128)(2,1)S(1)}, u32[]{:S(2)}, u32[]{:S(2)}) collective-permute-start(bf16[2,256,1536]{2,1,0:T(8,128)(2,1)S(1)} %get-tuple-element.32), channel_id=1, source_target_pairs={{0,4},{4,0},{8,12},{12,8},{16,20},{20,16},{24,28},{28,24},{1,5},{5... | collective-permute-start | bytes 4718600 | tf_op jit(solution)/shard_map/ppermute | solution.py:52
  61.4 15.7 %collective-permute-start.4 = (bf16[2,128,1024]{2,1,0:T(8,128)(2,1)S(1)}, bf16[2,128,1024]{2,1,0:T(8,128)(2,1)S(1)}, u32[]{:S(2)}, u32[]{:S(2)}) collective-permute-start(bf16[2,128,1024]{2,1,0:T(8,128)(2,1)S(1)} %add_convert_fusion.5.refs_8_.refs_9_), channel_id=1, source_target_pairs={{0,8},{4,20},{8,0},{12,28},{16,24},{20,4},{24,16},{28,12},{1,9},{5... | collective-permute-start | bytes 1572872 | tf_op jit(solution)/shard_map/ppermute | solution.py:49
  75.5 23.1 %collective-permute-start.9 = (bf16[2,256,2048]{2,1,0:T(8,128)(2,1)S(1)}, bf16[2,256,2048]{2,1,0:T(8,128)(2,1)S(1)}, u32[]{:S(2)}, u32[]{:S(2)}) collective-permute-start(bf16[2,256,2048]{2,1,0:T(8,128)(2,1)S(1)} %get-tuple-element.34), channel_id=1, source_target_pairs={{0,4},{4,0},{8,12},{12,8},{16,20},{20,16},{24,28},{28,24},{1,5},{5... | collective-permute-start | bytes 6291464 | tf_op jit(solution)/shard_map/ppermute | solution.py:52
  75.8 14.8 %collective-permute-start.7 = (bf16[2,128,1536]{2,1,0:T(8,128)(2,1)S(1)}, bf16[2,128,1536]{2,1,0:T(8,128)(2,1)S(1)}, u32[]{:S(2)}, u32[]{:S(2)}) collective-permute-start(bf16[2,128,1536]{2,1,0:T(8,128)(2,1)S(1)} %add_convert_fusion.2.refs_9_.refs_10_), channel_id=1, source_target_pairs={{0,8},{4,20},{8,0},{12,28},{16,24},{20,4},{24,16},{28,12},{1,9},{5... | collective-permute-start | bytes 2359304 | tf_op jit(solution)/shard_map/ppermute | solution.py:49
  90.0 9.6 %collective-permute-start.10 = (bf16[2,256,2048]{2,1,0:T(8,128)(2,1)S(1)}, bf16[2,256,2048]{2,1,0:T(8,128)(2,1)S(1)}, u32[]{:S(2)}, u32[]{:S(2)}) collective-permute-start(bf16[2,256,2048]{2,1,0:T(8,128)(2,1)S(1)} %get-tuple-element.37), channel_id=1, source_target_pairs={{0,4},{4,0},{8,12},{12,8},{16,20},{20,16},{24,28},{28,24},{1,5},{5... | collective-permute-start | bytes 6291464 | tf_op jit(solution)/shard_map/ppermute | solution.py:52
  91.3 10.6 %collective-permute-start.5 = (bf16[2,64,1024]{2,1,0:T(8,128)(2,1)S(1)}, bf16[2,64,1024]{2,1,0:T(8,128)(2,1)S(1)}, u32[]{:S(2)}, u32[]{:S(2)}) collective-permute-start(bf16[2,64,1024]{2,1,0:T(8,128)(2,1)S(1)} %add_convert_fusion.10.refs_8_), channel_id=1, source_target_pairs={{0,16},{4,12},{8,24},{12,4},{16,0},{20,28},{24,8},{28,20},{1,17},{... | collective-permute-start | bytes 786440 | tf_op jit(solution)/shard_map/ppermute | solution.py:49
  99.0 29.4 %collective-permute-start.11 = (bf16[2,128,2048]{2,1,0:T(8,128)(2,1)S(1)}, bf16[2,128,2048]{2,1,0:T(8,128)(2,1)S(1)}, u32[]{:S(2)}, u32[]{:S(2)}) collective-permute-start(bf16[2,128,2048]{2,1,0:T(8,128)(2,1)S(1)} %add_convert_fusion.1.refs_11_), channel_id=1, source_target_pairs={{0,8},{4,20},{8,0},{12,28},{16,24},{20,4},{24,16},{28,12},{1,9},{5... | collective-permute-start | bytes 3145736 | tf_op jit(solution)/shard_map/ppermute | solution.py:49
  103.0 24.9 %collective-permute-start.16 = (bf16[2,64,2560]{2,1,0:T(8,128)(2,1)S(1)}, bf16[2,64,2560]{2,1,0:T(8,128)(2,1)S(1)}, u32[]{:S(2)}, u32[]{:S(2)}) collective-permute-start(bf16[2,64,2560]{2,1,0:T(8,128)(2,1)S(1)} %get-tuple-element.39.refs_9_.refs_0_), channel_id=1, source_target_pairs={{0,8},{4,20},{8,0},{12,28},{16,24},{20,4},{24,16},{28,12},{1,9},{5... | collective-permute-start | bytes 1966088 | tf_op jit(solution)/shard_map/ppermute | solution.py:49
  103.3 45.5 %collective-permute-start.13 = (bf16[2,128,2048]{2,1,0:T(8,128)(2,1)S(1)}, bf16[2,128,2048]{2,1,0:T(8,128)(2,1)S(1)}, u32[]{:S(2)}, u32[]{:S(2)}) collective-permute-start(bf16[2,128,2048]{2,1,0:T(8,128)(2,1)S(1)} %add_convert_fusion.refs_12_), channel_id=1, source_target_pairs={{0,8},{4,20},{8,0},{12,28},{16,24},{20,4},{24,16},{28,12},{1,9},{5... | collective-permute-start | bytes 3145736 | tf_op jit(solution)/shard_map/ppermute | solution.py:49
  105.1 25.1 %collective-permute-start.15 = (bf16[2,64,2560]{2,1,0:T(8,128)(2,1)S(1)}, bf16[2,64,2560]{2,1,0:T(8,128)(2,1)S(1)}, u32[]{:S(2)}, u32[]{:S(2)}) collective-permute-start(bf16[2,64,2560]{2,1,0:T(8,128)(2,1)S(1)} %get-tuple-element.39.refs_9_.refs_0_), channel_id=1, source_target_pairs={{0,16},{4,12},{8,24},{12,4},{16,0},{20,28},{24,8},{28,20},{1,17},{... | collective-permute-start | bytes 1966088 | tf_op jit(solution)/shard_map/ppermute | solution.py:49
  127.9 20.9 %collective-permute-start.17 = (bf16[2,64,2560]{2,1,0:T(8,128)(2,1)S(1)}, bf16[2,64,2560]{2,1,0:T(8,128)(2,1)S(1)}, u32[]{:S(2)}, u32[]{:S(2)}) collective-permute-start(bf16[2,64,2560]{2,1,0:T(8,128)(2,1)S(1)} %collective-permute-done.16.refs_2_), channel_id=1, source_target_pairs={{0,16},{4,12},{8,24},{12,4},{16,0},{20,28},{24,8},{28,20},{1,17},{... | collective-permute-start | bytes 1966088 | tf_op jit(solution)/shard_map/ppermute | solution.py:49
  128.6 21.9 %collective-permute-start.12 = (bf16[2,64,2048]{2,1,0:T(8,128)(2,1)S(1)}, bf16[2,64,2048]{2,1,0:T(8,128)(2,1)S(1)}, u32[]{:S(2)}, u32[]{:S(2)}) collective-permute-start(bf16[2,64,2048]{2,1,0:T(8,128)(2,1)S(1)} %add_convert_fusion.4), channel_id=1, source_target_pairs={{0,16},{4,12},{8,24},{12,4},{16,0},{20,28},{24,8},{28,20},{1,17},{... | collective-permute-start | bytes 1572872 | tf_op jit(solution)/shard_map/ppermute | solution.py:49
  130.2 31.5 %collective-permute-start.18 = (bf16[2,64,2560]{2,1,0:T(8,128)(2,1)S(1)}, bf16[2,64,2560]{2,1,0:T(8,128)(2,1)S(1)}, u32[]{:S(2)}, u32[]{:S(2)}) collective-permute-start(bf16[2,64,2560]{2,1,0:T(8,128)(2,1)S(1)} %get-tuple-element.39.refs_9_.refs_0_), channel_id=1, source_target_pairs={{0,4},{4,0},{8,12},{12,8},{16,20},{20,16},{24,28},{28,24},{1,5},{5... | collective-permute-start | bytes 1966088 | tf_op jit(solution)/shard_map/ppermute | solution.py:52
  130.2 32.9 %collective-permute-start.20 = (bf16[2,64,2560]{2,1,0:T(8,128)(2,1)S(1)}, bf16[2,64,2560]{2,1,0:T(8,128)(2,1)S(1)}, u32[]{:S(2)}, u32[]{:S(2)}) collective-permute-start(bf16[2,64,2560]{2,1,0:T(8,128)(2,1)S(1)} %collective-permute-done.16.refs_2_), channel_id=1, source_target_pairs={{0,4},{4,0},{8,12},{12,8},{16,20},{20,16},{24,28},{28,24},{1,5},{5... | collective-permute-start | bytes 1966088 | tf_op jit(solution)/shard_map/ppermute | solution.py:52
  148.8 14.3 %collective-permute-start.19 = (bf16[2,64,2560]{2,1,0:T(8,128)(2,1)S(1)}, bf16[2,64,2560]{2,1,0:T(8,128)(2,1)S(1)}, u32[]{:S(2)}, u32[]{:S(2)}) collective-permute-start(bf16[2,64,2560]{2,1,0:T(8,128)(2,1)S(1)} %collective-permute-done.15.refs_1_), channel_id=1, source_target_pairs={{0,4},{4,0},{8,12},{12,8},{16,20},{20,16},{24,28},{28,24},{1,5},{5... | collective-permute-start | bytes 1966088 | tf_op jit(solution)/shard_map/ppermute | solution.py:52
  148.8 14.3 %collective-permute-start.21 = (bf16[2,64,2560]{2,1,0:T(8,128)(2,1)S(1)}, bf16[2,64,2560]{2,1,0:T(8,128)(2,1)S(1)}, u32[]{:S(2)}, u32[]{:S(2)}) collective-permute-start(bf16[2,64,2560]{2,1,0:T(8,128)(2,1)S(1)} %collective-permute-done.17.refs_3_), channel_id=1, source_target_pairs={{0,4},{4,0},{8,12},{12,8},{16,20},{20,16},{24,28},{28,24},{1,5},{5... | collective-permute-start | bytes 1966088 | tf_op jit(solution)/shard_map/ppermute | solution.py:52
  150.5 9.2 %collective-permute-start.14 = (bf16[2,64,2048]{2,1,0:T(8,128)(2,1)S(1)}, bf16[2,64,2048]{2,1,0:T(8,128)(2,1)S(1)}, u32[]{:S(2)}, u32[]{:S(2)}) collective-permute-start(bf16[2,64,2048]{2,1,0:T(8,128)(2,1)S(1)} %add_convert_fusion.3), channel_id=1, source_target_pairs={{0,16},{4,12},{8,24},{12,4},{16,0},{20,28},{24,8},{28,20},{1,17},{... | collective-permute-start | bytes 1572872 | tf_op jit(solution)/shard_map/ppermute | solution.py:49
  161.2 25.5 %collective-permute-start.23 = (bf16[2,64,4096]{2,1,0:T(8,128)(2,1)S(1)}, bf16[2,64,4096]{2,1,0:T(8,128)(2,1)S(1)}, u32[]{:S(2)}, u32[]{:S(2)}) collective-permute-start(bf16[2,64,4096]{2,1,0:T(8,128)(2,1)S(1)} %get-tuple-element.42.refs_12_.refs_0_), channel_id=1, source_target_pairs={{0,8},{4,20},{8,0},{12,28},{16,24},{20,4},{24,16},{28,12},{1,9},{5... | collective-permute-start | bytes 3145736 | tf_op jit(solution)/shard_map/ppermute | solution.py:49
  161.8 26.2 %collective-permute-start.22 = (bf16[2,64,4096]{2,1,0:T(8,128)(2,1)S(1)}, bf16[2,64,4096]{2,1,0:T(8,128)(2,1)S(1)}, u32[]{:S(2)}, u32[]{:S(2)}) collective-permute-start(bf16[2,64,4096]{2,1,0:T(8,128)(2,1)S(1)} %get-tuple-element.42.refs_12_.refs_0_), channel_id=1, source_target_pairs={{0,16},{4,12},{8,24},{12,4},{16,0},{20,28},{24,8},{28,20},{1,17},{... | collective-permute-start | bytes 3145736 | tf_op jit(solution)/shard_map/ppermute | solution.py:49
  186.6 14.8 %collective-permute-start.24 = (bf16[2,64,4096]{2,1,0:T(8,128)(2,1)S(1)}, bf16[2,64,4096]{2,1,0:T(8,128)(2,1)S(1)}, u32[]{:S(2)}, u32[]{:S(2)}) collective-permute-start(bf16[2,64,4096]{2,1,0:T(8,128)(2,1)S(1)} %collective-permute-done.23.refs_2_), channel_id=1, source_target_pairs={{0,16},{4,12},{8,24},{12,4},{16,0},{20,28},{24,8},{28,20},{1,17},{... | collective-permute-start | bytes 3145736 | tf_op jit(solution)/shard_map/ppermute | solution.py:49
  187.5 14.0 %collective-permute-start.25 = (bf16[2,64,4096]{2,1,0:T(8,128)(2,1)S(1)}, bf16[2,64,4096]{2,1,0:T(8,128)(2,1)S(1)}, u32[]{:S(2)}, u32[]{:S(2)}) collective-permute-start(bf16[2,64,4096]{2,1,0:T(8,128)(2,1)S(1)} %get-tuple-element.42.refs_12_.refs_0_), channel_id=1, source_target_pairs={{0,4},{4,0},{8,12},{12,8},{16,20},{20,16},{24,28},{28,24},{1,5},{5... | collective-permute-start | bytes 3145736 | tf_op jit(solution)/shard_map/ppermute | solution.py:52
  187.5 14.0 %collective-permute-start.27 = (bf16[2,64,4096]{2,1,0:T(8,128)(2,1)S(1)}, bf16[2,64,4096]{2,1,0:T(8,128)(2,1)S(1)}, u32[]{:S(2)}, u32[]{:S(2)}) collective-permute-start(bf16[2,64,4096]{2,1,0:T(8,128)(2,1)S(1)} %collective-permute-done.23.refs_2_), channel_id=1, source_target_pairs={{0,4},{4,0},{8,12},{12,8},{16,20},{20,16},{24,28},{28,24},{1,5},{5... | collective-permute-start | bytes 3145736 | tf_op jit(solution)/shard_map/ppermute | solution.py:52
  188.0 13.5 %collective-permute-start.26 = (bf16[2,64,4096]{2,1,0:T(8,128)(2,1)S(1)}, bf16[2,64,4096]{2,1,0:T(8,128)(2,1)S(1)}, u32[]{:S(2)}, u32[]{:S(2)}) collective-permute-start(bf16[2,64,4096]{2,1,0:T(8,128)(2,1)S(1)} %collective-permute-done.22.refs_1_), channel_id=1, source_target_pairs={{0,4},{4,0},{8,12},{12,8},{16,20},{20,16},{24,28},{28,24},{1,5},{5... | collective-permute-start | bytes 3145736 | tf_op jit(solution)/shard_map/ppermute | solution.py:52
  218.7 19.7 %collective-permute-start.29 = (bf16[128,1024]{1,0:T(8,128)(2,1)S(1)}, bf16[128,1024]{1,0:T(8,128)(2,1)S(1)}, u32[]{:S(2)}, u32[]{:S(2)}) collective-permute-start(bf16[128,1024]{1,0:T(8,128)(2,1)S(1)} %get-tuple-element.46), channel_id=1, source_target_pairs={{0,3},{1,2},{2,1},{3,0},{4,7},{5,6},{6,5},{7,4},{8,11},{9,10},{10,... | collective-permute-start | bytes 786440 | tf_op jit(solution)/shard_map/ppermute | solution.py:337
  223.2 22.3 %collective-permute-start.30 = (bf16[128,1024]{1,0:T(8,128)(2,1)S(1)}, bf16[128,1024]{1,0:T(8,128)(2,1)S(1)}, u32[]{:S(2)}, u32[]{:S(2)}) collective-permute-start(bf16[128,1024]{1,0:T(8,128)(2,1)S(1)} %get-tuple-element.47), channel_id=1, source_target_pairs={{0,2},{1,3},{2,0},{3,1},{4,6},{5,7},{6,4},{7,5},{8,10},{9,11},{10,... | collective-permute-start | bytes 786440 | tf_op jit(solution)/shard_map/ppermute | solution.py:337
  223.2 22.3 %collective-permute-start.31 = (bf16[128,1024]{1,0:T(8,128)(2,1)S(1)}, bf16[128,1024]{1,0:T(8,128)(2,1)S(1)}, u32[]{:S(2)}, u32[]{:S(2)}) collective-permute-start(bf16[128,1024]{1,0:T(8,128)(2,1)S(1)} %get-tuple-element.48), channel_id=1, source_target_pairs={{0,1},{1,0},{2,3},{3,2},{4,5},{5,4},{6,7},{7,6},{8,9},{9,8},{10,11... | collective-permute-start | bytes 786440 | tf_op jit(solution)/shard_map/ppermute | solution.py:337
  253.4 13.5 %collective-permute-start.33 = (bf16[128,1024]{1,0:T(8,128)(2,1)S(1)}, bf16[128,1024]{1,0:T(8,128)(2,1)S(1)}, u32[]{:S(2)}, u32[]{:S(2)}) collective-permute-start(bf16[128,1024]{1,0:T(8,128)(2,1)S(1)} %add_convert_fusion.8), channel_id=1, source_target_pairs={{0,2},{1,3},{2,0},{3,1},{4,6},{5,7},{6,4},{7,5},{8,10},{9,11},{10,... | collective-permute-start | bytes 786440 | tf_op jit(solution)/shard_map/ppermute | solution.py:337
  254.6 12.3 %collective-permute-start.34 = (bf16[128,1024]{1,0:T(8,128)(2,1)S(1)}, bf16[128,1024]{1,0:T(8,128)(2,1)S(1)}, u32[]{:S(2)}, u32[]{:S(2)}) collective-permute-start(bf16[128,1024]{1,0:T(8,128)(2,1)S(1)} %get-tuple-element.55), channel_id=1, source_target_pairs={{0,1},{1,0},{2,3},{3,2},{4,5},{5,4},{6,7},{7,6},{8,9},{9,8},{10,11... | collective-permute-start | bytes 786440 | tf_op jit(solution)/shard_map/ppermute | solution.py:337
  (7 other events, 44.4 us)
